TPU v7x, 32 devices: a whole 2x2x4 slice. The times are simulated.
32 devices in a mesh: dp: 2 (over x), expert: 16 (over z, y, core).
Axes of the slice: x: 2, y: 2, z: 4, core: 2. Of those that a mesh axis runs over, the one named last changes fastest.
Arguments:
- tokens: bfloat16 [2048, 4096], P('expert', 'dp'), may hold values from -6 to 6
- expert_ids: int32 [2048, 8], P('expert'), may hold values from 0 to 15, all different within a row; in each aligned block of 128 rows (0 to 127, 128 to 255, ...) at most 70 rows name the same one
- route_weight: float32 [2048, 8], P('expert'), may hold values from 0.1 to 1
- placement: int32 [16], replicated, may hold values from 0 to 15, each once
- swap_flag: int32 [8], replicated, may hold values 0 or 1
- gate_up: bfloat16 [16, 2, 768, 4096], P('expert', None, 'dp'), may hold values from -0.09375 to 0.09375
- down_weight: bfloat16 [16, 768, 4096], P('expert', None, 'dp'), may hold values from -0.21875 to 0.21875
Outputs:
- moe_out: bfloat16 [2048, 4096], P('expert', 'dp')
- column_load: float32 [16], replicated
- slot_gate_up: bfloat16 [16, 2, 768, 4096], P('expert', None, 'dp')
- slot_down: bfloat16 [16, 768, 4096], P('expert', None, 'dp')
Inputs may be any that keep to these rules, and one draw needn't show every extreme that they name: `expert_ids`: within the rows of one device (aligned blocks of 128 tokens) no expert is chosen more than 70 times, and some expert is chosen exactly 70 times; a token's 8 experts differ. A permutation: expert e's weights are in slot placement[e]. swap_flag[p] = 1 means slots p and p + 8 exchange owners.
All inputs are finite; a program needn't handle non-finite values.
Results may differ from a plain program's by a relative error of at most 0.0057.
Values may be sent and summed in bfloat16 or wider, within the bound.
No kernel may reach another device: no remote copies, remote signals or barrier semaphores. Data moves between devices by JAX's collectives and lax.ppermute only.
A program may use at most 128 MiB of HBM per device.

v0:
```python
import jax
import jax.numpy as jnp
from jax import lax
from jax.experimental import pallas as pl
from jax.experimental.pallas import tpu as pltpu
from jax.sharding import Mesh
from jax.sharding import PartitionSpec as P

COLUMN = ("z", "y", "core")


def project_kernel(part_ref, x_ref, own_w_ref, other_w_ref, out_ref):
    blocks, rows, feat = x_ref.shape[1:]
    hid = out_ref.shape[1]
    contract = (((1,), (1,)), ((), ()))
    total = lax.dot_general(
        x_ref[0].reshape(blocks * rows, feat),
        own_w_ref[...],
        contract,
        preferred_element_type=jnp.float32,
    )
    total += lax.dot_general(
        x_ref[1].reshape(blocks * rows, feat),
        other_w_ref[...],
        contract,
        preferred_element_type=jnp.float32,
    )
    gate, up = total[:, :hid], total[:, hid:]
    out_ref[...] = (gate / (1.0 + jnp.exp(-gate)) * up).astype(jnp.bfloat16)


def project(part, x_all, w_pair, step):
    blocks, rows, feat = x_all.shape[1:]
    hid2, width = w_pair.shape
    hid = hid2 // 2
    return pl.pallas_call(
        project_kernel,
        grid_spec=pltpu.PrefetchScalarGridSpec(
            num_scalar_prefetch=1,
            grid=(blocks // step,),
            in_specs=[
                pl.BlockSpec((2, step, rows, feat), lambda i, part: (0, i, 0, 0)),
                pl.BlockSpec((hid2, feat), lambda i, part: (0, part[0])),
                pl.BlockSpec((hid2, feat), lambda i, part: (0, 1 - part[0])),
            ],
            out_specs=pl.BlockSpec((step * rows, hid), lambda i, part: (i, 0)),
        ),
        out_shape=jax.ShapeDtypeStruct((blocks * rows, hid), jnp.bfloat16),
        compiler_params=pltpu.CompilerParams(vmem_limit_bytes=48 << 20),
        cost_estimate=pl.CostEstimate(
            flops=2 * blocks * rows * hid2 * width,
            bytes_accessed=2 * (blocks * rows * width + hid2 * width),
            transcendentals=blocks * rows * hid,
        ),
        name="project",
    )(part, x_all, w_pair, w_pair)


def down_kernel(part_ref, own_ref, other_ref, own_w_ref, other_w_ref, scale_ref, out_ref):
    result = jnp.dot(own_ref[...], own_w_ref[...], preferred_element_type=jnp.float32)
    result += jnp.dot(other_ref[...], other_w_ref[...], preferred_element_type=jnp.float32)
    result = result.astype(jnp.bfloat16).astype(jnp.float32)
    out_ref[...] = (result * scale_ref[...]).astype(out_ref.dtype)


def down(part, own, other, w_down, scale, block):
    rows, hid = own.shape
    depth, feat = w_down.shape
    return pl.pallas_call(
        down_kernel,
        grid_spec=pltpu.PrefetchScalarGridSpec(
            num_scalar_prefetch=1,
            grid=(rows // block,),
            in_specs=[
                pl.BlockSpec((block, hid), lambda i, part: (i, 0)),
                pl.BlockSpec((block, hid), lambda i, part: (i, 0)),
                pl.BlockSpec((hid, feat), lambda i, part: (part[0], 0)),
                pl.BlockSpec((hid, feat), lambda i, part: (1 - part[0], 0)),
                pl.BlockSpec((block, 1), lambda i, part: (i, 0)),
            ],
            out_specs=pl.BlockSpec((block, feat), lambda i, part: (i, 0)),
        ),
        out_shape=jax.ShapeDtypeStruct((rows, feat), jnp.bfloat16),
        compiler_params=pltpu.CompilerParams(vmem_limit_bytes=48 << 20),
        cost_estimate=pl.CostEstimate(
            flops=2 * rows * depth * feat,
            bytes_accessed=2 * (rows * depth + depth * feat + rows * feat),
            transcendentals=0,
        ),
        name="down",
    )(part, own, other, w_down, w_down, scale)


def hop(value, axis, mask=1):
    return lax.ppermute(value, axis, [(p, p ^ mask) for p in range(lax.axis_size(axis))])


def tie(*values):
    return lax.optimization_barrier(values)


def wide(value):
    return value.astype(jnp.float32)


def serve(hidden_own, cross_own, hidden_other, cross_other, w_down, scale):
    part = lax.axis_index("dp").astype(jnp.int32).reshape(1)
    rows = hidden_own.shape[0] // 4
    feat = w_down.shape[1]
    sent = down(part, hidden_other, cross_other, w_down, scale[1], 2 * rows)
    received = hop(sent, "core")
    kept = down(part, hidden_own, cross_own, w_down, scale[0], 2 * rows)
    return [v.reshape(2, 2, rows, feat) for v in (kept, received)]


def across_y(kept, received):
    leave = (wide(kept[1]) + wide(received[1])).astype(jnp.bfloat16)
    return wide(kept[0]) + wide(received[0]), hop(leave, "y")


def gather_stage(tokens, near, far, apart, across_0, beside_0, across_2, beside_2, table, tail, w_pair):
    rows = tokens.shape[0]
    part = lax.axis_index("dp").astype(jnp.int32).reshape(1)
    mine = jnp.arange(table.shape[1], dtype=jnp.int32) == lax.axis_index(COLUMN)
    across_3, beside_3, corner_2, table_y, near = tie(
        hop(apart, "dp"), hop(apart, "y"), hop(beside_2, "dp"), hop(table, "y"), near
    )
    table = jnp.concatenate([table, table_y])
    corner_3, across_1, beside_1, table_core, across_0, tail = tie(
        hop(across_3, "y"), hop(near, "dp"), hop(near, "y"), hop(table, "core"), across_0, tail
    )
    table = jnp.concatenate([table, table_core])
    own = jnp.stack([far, apart, beside_2, beside_3])
    x_late = jnp.stack([own, jnp.stack([across_2, across_3, corner_2, corner_3])])
    x_late_other = hop(x_late, "core")
    counts = jnp.sum((table >= 0).astype(jnp.float32), axis=(0, 2))
    scale = jnp.sum(jnp.where(mine[None, :, None], jnp.maximum(table, 0.0), 0.0), axis=1)
    scale = scale.reshape(2, 2, 2, 2, rows).transpose(0, 3, 1, 2, 4)
    scale = scale.reshape(2, 2, 4 * rows, 1)
    corner_0, corner_1 = hop(across_0, "y"), hop(beside_1, "dp")
    late_own = project(part, x_late, w_pair, 4)
    late_other = project(part, x_late_other, w_pair, 4)
    corner_0, corner_1, late_own, late_other, scale, tail = tie(
        corner_0, corner_1, late_own, late_other, scale, hop(tail, "core")
    )
    own = jnp.stack([tokens, near, beside_0, beside_1])
    x_early = jnp.stack([own, jnp.stack([across_0, across_1, corner_0, corner_1])])
    return x_early, late_own, hop(late_own, "dp"), late_other, scale, counts, tail


def expert_stage(x_early, late_own, late_own_cross, late_other, scale, w_pair, w_down):
    part = lax.axis_index("dp").astype(jnp.int32).reshape(1)
    late_other_cross = hop(late_other, "dp")
    x_early_other = hop(x_early, "core")
    early_own = project(part, x_early, w_pair, 4)
    early_own_cross = hop(early_own, "dp")
    late_other, early_own = tie(late_other, early_own)
    late = serve(late_own, late_own_cross, late_other, late_other_cross, w_down, scale[:, 1])
    early_other = project(part, x_early_other, w_pair, 4)
    early_other_cross = hop(early_other, "dp")
    line, line_y = across_y(*late)
    line = (line + wide(line_y)).astype(jnp.bfloat16)
    early = serve(early_own, early_own_cross, early_other, early_other_cross, w_down, scale[:, 0])
    total, total_y = across_y(*early)
    return line, total + wide(total_y)


def guarded(valid, stage, *operands):
    shapes = jax.eval_shape(stage, *operands)
    empty = lambda *_: jax.tree.map(lambda leaf: jnp.zeros(leaf.shape, leaf.dtype), shapes)
    return lax.cond(valid, stage, empty, *operands)


def body(tokens, expert_ids, route_weight, placement, swap_flag, gate_up, down_weight):
    ncol = lax.axis_size(COLUMN)
    half = ncol // 2
    rows = tokens.shape[0]
    topk = expert_ids.shape[1]
    hid = gate_up.shape[2]
    width = gate_up.shape[3]
    me = lax.axis_index(COLUMN)
    core = lax.axis_index("core")
    w_pair = gate_up.reshape(2 * hid, width)
    w_down = down_weight.reshape(down_weight.shape[1:])
    depth = w_down.shape[0] // 2

    slots = jnp.arange(ncol, dtype=jnp.int32)
    own = jnp.sum(jnp.where(slots[:half] == me % half, swap_flag, 0)) == 1
    sibling = jnp.sum(jnp.where(slots[:half] == (me + 1 - 2 * core) % half, swap_flag, 0)) == 1
    alone = own & ~sibling
    both = own & sibling

    picks = expert_ids[:, :, None] == jnp.arange(placement.shape[0], dtype=jnp.int32)
    slot = jnp.sum(jnp.where(picks, placement, 0), axis=2)
    here = slot[:, :, None] == slots
    named = jnp.any(here, axis=1)
    weight = jnp.sum(jnp.where(here, route_weight[:, :, None], 0.0), axis=1)
    table = jnp.where(named, weight, -1.0).T[None]

    heads, tails = (w_pair[:hid], w_down[:depth]), (w_pair[hid:], w_down[depth:])
    far, near, across_0, beside_0, table_far, late_tail = tie(
        hop(tokens, "z", 2),
        hop(tokens, "z", 1),
        hop(tokens, "dp"),
        hop(tokens, "y"),
        hop(table, "z", 2),
        tails[0],
    )
    table = jnp.concatenate([table, table_far])
    lane_pair = jnp.where(own, heads[0], hop(late_tail, "core"))
    apart, across_2, beside_2, table_near, lane_pair = tie(
        hop(far, "z", 1),
        hop(far, "dp"),
        hop(far, "y"),
        hop(table, "z", 1),
        lane_pair,
    )
    table = jnp.concatenate([table, table_near])
    mark = 2 * hid // 3
    arrived_first = hop(lane_pair[:mark], "z", 2)

    valid = placement[0] >= 0
    planes = (tokens, near, far, apart, across_0, beside_0, across_2, beside_2)
    *staged, counts, tail_down = guarded(valid, gather_stage, *planes, table, tails[1], w_pair)
    lane_down = jnp.where(own, heads[1], tail_down)
    *staged, arrived_first, lane_second, lane_down = tie(
        *staged, arrived_first, lane_pair[mark:], lane_down
    )
    arrived_second, arrived_down = hop(lane_second, "z", 2), hop(lane_down, "z", 2)
    handed_first = hop(arrived_first, "core")
    line, total = guarded(valid, expert_stage, *staged, w_pair, w_down)
    line, total, arrived_second, arrived_down = tie(line, total, arrived_second, arrived_down)
    line = (wide(line[0]) + wide(hop(line[1], "z", 1))).astype(jnp.bfloat16)
    closing = hop(total[1].astype(jnp.bfloat16), "z", 1)
    over, closing, *last = tie(hop(line, "z", 2), closing, *tails)
    handed_down, handed_second = hop(arrived_down, "core"), hop(arrived_second, "core")
    moe_out = (total[0] + wide(closing) + wide(over)).astype(jnp.bfloat16)
    partner = (slots + half * jnp.tile(swap_flag, 2)) % ncol
    column_load = jnp.sum(
        jnp.where(partner[:, None] == slots[None, :], counts[None, :], 0.0), axis=1
    ) / jnp.float32(rows * topk)

    rest = lax.cond(
        both, lambda a, b: (hop(a, "z", 2), hop(b, "z", 2)), lambda a, b: (a, b), *last
    )
    arrived = (jnp.concatenate([arrived_first, arrived_second]), arrived_down)
    handed = (jnp.concatenate([handed_first, handed_second]), handed_down)
    heads = [jnp.where(own, new, old) for new, old in zip(arrived, heads)]
    tails = [jnp.where(alone, new, old) for new, old in zip(handed, rest)]
    slot_gate_up = jnp.stack([heads[0], tails[0]])[None]
    slot_down = jnp.concatenate([heads[1], tails[1]])[None]
    return (moe_out, column_load, slot_gate_up, slot_down)


def from_behind(value, axis, steps):
    count = lax.axis_size(axis)
    pairs = [(source, (source + steps) % count) for source in range(count)]
    return lax.ppermute(value, axis, pairs)


def swapped_blocks(gate_up, down_weight, swap_flag, pair_index, half):
    incoming_pair = from_behind(gate_up, "expert", half)
    incoming_down = from_behind(down_weight, "expert", half)
    own_column = lax.axis_index("expert")
    own_flag = jnp.sum(jnp.where(pair_index == own_column % half, swap_flag, 0))
    pair_after = jnp.where(own_flag == 1, incoming_pair, gate_up)
    down_after = jnp.where(own_flag == 1, incoming_down, down_weight)
    return (pair_after, down_after)


def dispatched_body(tokens, expert_ids, route_weight, placement, swap_flag, gate_up, down_weight):
    ncol = lax.axis_size("expert")
    half = ncol // 2
    rows_here, feat_here = tokens.shape
    topk = expert_ids.shape[1]
    hid_here = gate_up.shape[2]
    width = gate_up.shape[3]
    capacity = max(4, rows_here * topk * 17 // (16 * ncol) + 2)
    experts_all = placement.shape[0]
    pair_index = jnp.arange(half, dtype=jnp.int32)
    hits = placement[:, None] % half == pair_index[None, :]
    flag_of = jnp.sum(jnp.where(hits, swap_flag[None, :], 0), axis=1)
    moved = (placement + half * flag_of) % ncol
    picks = expert_ids.reshape(-1)[:, None] == jnp.arange(experts_all, dtype=jnp.int32)[None, :]
    moved_dest = jnp.sum(jnp.where(picks, moved[None, :], 0), axis=1)
    columns = jnp.arange(ncol, dtype=jnp.int32)
    local_counts = jnp.sum((moved_dest[:, None] == columns[None, :]).astype(jnp.float32), axis=0)
    totals = lax.psum(local_counts, "expert")
    column_load = totals / jnp.float32(rows_here * topk)
    slot_gate_up, slot_down = swapped_blocks(gate_up, down_weight, swap_flag, pair_index, half)
    col_hits = moved_dest[:, None] == columns[None, :]
    order = jnp.cumsum(col_hits.astype(jnp.int32), axis=0) - 1
    position = jnp.sum(jnp.where(col_hits, order, 0), axis=1)
    slot_index = moved_dest * capacity + position
    w_pair = slot_gate_up.reshape(2 * hid_here, width)
    w_down = slot_down.reshape(slot_down.shape[1], feat_here)
    contract = (((1,), (1,)), ((), ()))
    whole = lax.all_gather(tokens, "dp", axis=1, tiled=True)
    repeated = jnp.repeat(whole, topk, axis=0)
    buffer = jnp.zeros((ncol * capacity, width), jnp.bfloat16).at[slot_index].set(repeated)
    buffer = buffer.reshape(ncol, capacity, width)
    received = lax.all_to_all(buffer, "expert", split_axis=0, concat_axis=0, tiled=True)
    blocks, count, wide = received.shape
    rows = received.reshape(blocks * count, wide)
    projected = lax.dot_general(rows, w_pair, contract, preferred_element_type=jnp.float32)
    hidden = (jax.nn.silu(projected[:, :hid_here]) * projected[:, hid_here:]).astype(jnp.bfloat16)
    mixed = jnp.dot(
        lax.all_gather(hidden, "dp", axis=1, tiled=True), w_down, preferred_element_type=jnp.float32
    )
    result = mixed.astype(jnp.bfloat16).reshape(blocks, count, feat_here)
    returned = lax.all_to_all(result, "expert", split_axis=0, concat_axis=0, tiled=True)
    flat_back = returned.reshape(ncol * capacity, feat_here)
    gathered = flat_back[slot_index].astype(jnp.float32).reshape(rows_here, topk, feat_here)
    moe_out = jnp.sum(gathered * route_weight[:, :, None], axis=1).astype(jnp.bfloat16)
    return (moe_out, column_load, slot_gate_up, slot_down)


def solution(mesh):
    expert = mesh.shape["expert"]
    if expert != 16 or mesh.shape["dp"] != 2:
        run, names, column = dispatched_body, mesh, "expert"
    else:
        shape = (mesh.shape["dp"], expert // 4, 2, 2)
        run, names, column = body, Mesh(mesh.devices.reshape(shape), ("dp", *COLUMN)), COLUMN
    return jax.shard_map(
        run,
        mesh=names,
        in_specs=(
            P(column, "dp"),
            P(column, None),
            P(column, None),
            P(),
            P(),
            P(column, None, "dp", None),
            P(column, None, "dp"),
        ),
        out_specs=(P(column, "dp"), P(), P(column, None, "dp", None), P(column, None, "dp")),
        check_vma=False,
    )
```

profile of v0, /device:TPU:24, one launch (start us, length us, event | category | flops | bytes accessed | tf_op | source)
XLA Modules:
  0.0 412.1 jit_solution(6817817974812328347)
XLA Ops:
  10.8 16.1 %collective-permute-done.27 = f32[1,16,128]{2,1,0:T(8,128)S(1)} collective-permute-done((f32[1,16,128]{2,1,0:T(8,128)S(1)}, f32[1,16,128]{2,1,0:T(8,128)S(1)}, u32[]{:S(2)}, u32[]{:S(2)}) %collective-permute-start.27) | collective-permute-done | bytes 8224 | tf_op jit(solution)/shard_map/ppermute | solution.py:95
  37.4 7.0 %collective-permute-done.31 = f32[2,16,128]{2,1,0:T(8,128)S(1)} collective-permute-done((f32[2,16,128]{2,1,0:T(8,128)S(1)}, f32[2,16,128]{2,1,0:T(8,128)S(1)}, u32[]{:S(2)}, u32[]{:S(2)}) %collective-permute-start.31) | collective-permute-done | bytes 16416 | tf_op jit(solution)/shard_map/ppermute | solution.py:95
  49.6 77.8 %conditional.3 = (bf16[2,4,128,2048]{3,2,1,0:T(8,128)(2,1)}, bf16[512,384]{1,0:T(8,128)(2,1)S(1)}, bf16[512,384]{1,0:T(8,128)(2,1)}, bf16[512,384]{1,0:T(8,128)(...) conditional(s32[]{:T(128)} %bitcast.36, () %tuple.41, ...), branch_computations={%region_4.5_spmd, %region_5.8_spmd} | conditional | flops 6459439104 | bytes 133833904 | solution.py:171
  53.8 9.5 %collective-permute-done.5 = f32[4,16,128]{2,1,0:T(8,128)S(1)} collective-permute-done((f32[4,16,128]{2,1,0:T(8,128)S(1)}, f32[4,16,128]{2,1,0:T(8,128)S(1)}, u32[]{:S(2)}, u32[]{:S(2)}) %collective-permute-start.5) | collective-permute-done | bytes 32800 | tf_op jit(solution)/shard_map/cond/branch_1_fun/ppermute | solution.py:95
  64.6 8.2 %collective-permute-done.4 = bf16[128,2048]{1,0:T(8,128)(2,1)S(1)} collective-permute-done((bf16[128,2048]{1,0:T(8,128)(2,1)S(1)}, bf16[128,2048]{1,0:T(8,128)(2,1)S(1)}, u32[]{:S(2)}, u32[]{:S(2)}) %collective-permute-start.4) | collective-permute-done | bytes 524320 | tf_op jit(solution)/shard_map/cond/branch_1_fun/ppermute | solution.py:95
  77.4 6.7 %collective-permute-done.7 = bf16[128,2048]{1,0:T(8,128)(2,1)S(1)} collective-permute-done((bf16[128,2048]{1,0:T(8,128)(2,1)S(1)}, bf16[128,2048]{1,0:T(8,128)(2,1)S(1)}, u32[]{:S(2)}, u32[]{:S(2)}) %collective-permute-start.7) | collective-permute-done | bytes 524320 | tf_op jit(solution)/shard_map/cond/branch_1_fun/ppermute | solution.py:95
  84.2 4.8 %collective-permute-done.8 = bf16[128,2048]{1,0:T(8,128)(2,1)S(1)} collective-permute-done((bf16[128,2048]{1,0:T(8,128)(2,1)S(1)}, bf16[128,2048]{1,0:T(8,128)(2,1)S(1)}, u32[]{:S(2)}, u32[]{:S(2)}) %collective-permute-start.8) | collective-permute-done | bytes 524320 | tf_op jit(solution)/shard_map/cond/branch_1_fun/ppermute | solution.py:95
  89.0 7.8 %collective-permute-done.6 = bf16[128,2048]{1,0:T(8,128)(2,1)S(1)} collective-permute-done((bf16[128,2048]{1,0:T(8,128)(2,1)S(1)}, bf16[128,2048]{1,0:T(8,128)(2,1)S(1)}, u32[]{:S(2)}, u32[]{:S(2)}) %collective-permute-start.6) | collective-permute-done | bytes 524320 | tf_op jit(solution)/shard_map/cond/branch_1_fun/ppermute | solution.py:95
  102.4 7.6 %project.4 = bf16[512,384]{1,0:T(8,128)(2,1)S(1)} custom-call(s32[1]{0:T(128)} %bitcast.7.part_ref, bf16[2,4,128,2048]{3,2,1,0:T(8,128)(2,1)} %pad_maximum_fusion.x_ref, bf16[768,4096]{1,0:T(8,128)(2,1)} %get-tuple-element.64.own_w_ref.other_w_ref, bf16[768,4096]{1,0:T(8,128)(2,1)} %get-tuple-element.64.own_w_ref.other_w_ref), custom_call_target="tpu_custom_call" | custom-call | flops 3221225472 | bytes 10485760 | tf_op jit(solution)/shard_map/cond/branch_1_fun/project/pallas_call | solution.py:36
  110.4 6.4 %project.5 = bf16[512,384]{1,0:T(8,128)(2,1)} custom-call(s32[1]{0:T(128)} %bitcast.7.part_ref, bf16[2,4,128,2048]{3,2,1,0:T(8,128)(2,1)} %collective-permute-done.12.x_ref, bf16[768,4096]{1,0:T(8,128)(2,1)S(1)} %bitcast.86, bf16[768,4096]{1,0:T(8,128)(2,1)S(1)} %bitcast.86), custom_call_target="tpu_custom_call" | custom-call | flops 3221225472 | bytes 10485760 | tf_op jit(solution)/shard_map/cond/branch_1_fun/project/pallas_call | solution.py:36
  122.8 4.7 %collective-permute-done.14 = bf16[512,384]{1,0:T(8,128)(2,1)} collective-permute-done((bf16[512,384]{1,0:T(8,128)(2,1)S(1)}, bf16[512,384]{1,0:T(8,128)(2,1)}, u32[]{:S(2)}, u32[]{:S(2)}) %collective-permute-start.14) | collective-permute-done | bytes 393248 | tf_op jit(solution)/shard_map/cond/branch_1_fun/ppermute | solution.py:95
  128.8 10.1 %collective-permute-done.33 = bf16[256,4096]{1,0:T(8,128)(2,1)} collective-permute-done((bf16[256,4096]{1,0:T(8,128)(2,1)}, bf16[256,4096]{1,0:T(8,128)(2,1)}, u32[]{:S(2)}, u32[]{:S(2)}) %collective-permute-start.33) | collective-permute-done | bytes 2097184 | tf_op jit(solution)/shard_map/ppermute | solution.py:95
  143.9 104.6 %conditional.4 = (bf16[2,128,2048]{2,1,0:T(8,128)(2,1)}, f32[2,128,2048]{2,1,0:T(8,128)}) conditional(s32[]{:T(128)} %bitcast.36, () %tuple.40, (bf16[1,768,2048]{2,1,0:T(8,128)(2,1)S(1)}, f32[2,2,512,1]{2,1,0,3:T(2,128)S(1)}, bf16[512,384]{1,0:T(8,128)(2,1)S(1)}, bf16[512,384]{1,0:T(8,128)(2,1)}, bf16[2,4,128,2048]{3,2,1,0:T(8,128)(2,1)}, ...), branch_computations={%region_8.9_spmd, %region_9.10_spmd} | conditional | flops 12894863360 | bytes 167821776 | solution.py:171
  146.9 7.5 %project.6.own_ref = bf16[512,384]{1,0:T(8,128)(2,1)S(1)} custom-call(s32[1]{0:T(128)} %bitcast.26.part_ref, bf16[2,4,128,2048]{3,2,1,0:T(8,128)(2,1)} %get-tuple-element.78.x_ref, bf16[768,4096]{1,0:T(8,128)(2,1)} %get-tuple-element.79.own_w_ref.other_w_ref, bf16[768,4096]{1,0:T(8,128)(2,1)} %get-tuple-element.79.own_w_ref.other_w_ref), custom_call_target="tpu_custom_call" | custom-call | flops 3221225472 | bytes 10485760 | tf_op jit(solution)/shard_map/cond/branch_1_fun/project/pallas_call | solution.py:36
  155.6 4.7 %down.5 = bf16[512,2048]{1,0:T(8,128)(2,1)S(1)} custom-call(s32[1]{0:T(128)} %bitcast.26.part_ref, bf16[512,384]{1,0:T(8,128)(2,1)} %get-tuple-element.80.own_ref, bf16[512,384]{1,0:T(8,128)(2,1)S(1)} %collective-permute-done.15.other_ref, bf16[768,2048]{1,0:T(8,128)(2,1)} %bitcast.87, bf16[768,2048]{1,0:T(8,128)(2,1)} %bitcast.88, f32[512,1]{1,0:T(8,128)S(1)} %copy.22.scale_ref), custom_call_target="tpu_custom_call" | custom-call | flops 1610612736 | bytes 6029312 | tf_op jit(solution)/shard_map/cond/branch_1_fun/down/pallas_call | solution.py:69
  160.4 5.6 %project.7.own_ref = bf16[512,384]{1,0:T(8,128)(2,1)S(1)} custom-call(s32[1]{0:T(128)} %bitcast.26.part_ref, bf16[2,4,128,2048]{3,2,1,0:T(8,128)(2,1)} %collective-permute-done.19.x_ref, bf16[768,4096]{1,0:T(8,128)(2,1)S(1)} %copy-done, bf16[768,4096]{1,0:T(8,128)(2,1)S(1)} %copy-done), custom_call_target="tpu_custom_call" | custom-call | flops 3221225472 | bytes 10485760 | tf_op jit(solution)/shard_map/cond/branch_1_fun/project/pallas_call | solution.py:36
  167.7 10.0 %collective-permute-done.20.other_ref = bf16[512,384]{1,0:T(8,128)(2,1)S(1)} collective-permute-done((bf16[512,384]{1,0:T(8,128)(2,1)S(1)}, bf16[512,384]{1,0:T(8,128)(2,1)S(1)}, u32[]{:S(2)}, u32[]{:S(2)}) %collective-permute-start.20) | collective-permute-done | bytes 393248 | tf_op jit(solution)/shard_map/cond/branch_1_fun/ppermute | solution.py:95
  177.7 5.4 %down.7 = bf16[512,2048]{1,0:T(8,128)(2,1)} custom-call(s32[1]{0:T(128)} %bitcast.26.part_ref, bf16[512,384]{1,0:T(8,128)(2,1)S(1)} %project.7.own_ref, bf16[512,384]{1,0:T(8,128)(2,1)S(1)} %collective-permute-done.20.other_ref, bf16[768,2048]{1,0:T(8,128)(2,1)} %bitcast.89, bf16[768,2048]{1,0:T(8,128)(2,1)} %bitcast.90, f32[512,1]{1,0:T(8,128)S(1)} %copy.24.scale_ref), custom_call_target="tpu_custom_call" | custom-call | flops 1610612736 | bytes 6029312 | tf_op jit(solution)/shard_map/cond/branch_1_fun/down/pallas_call | solution.py:69
  184.8 4.8 %down.4 = bf16[512,2048]{1,0:T(8,128)(2,1)S(1)} custom-call(s32[1]{0:T(128)} %bitcast.26.part_ref, bf16[512,384]{1,0:T(8,128)(2,1)} %copy-done.11, bf16[512,384]{1,0:T(8,128)(2,1)} %get-tuple-element.74.other_ref, bf16[768,2048]{1,0:T(8,128)(2,1)} %bitcast.91, bf16[768,2048]{1,0:T(8,128)(2,1)} %bitcast.92, f32[512,1]{1,0:T(8,128)S(1)} %copy.21.scale_ref), custom_call_target="tpu_custom_call" | custom-call | flops 1610612736 | bytes 6029312 | tf_op jit(solution)/shard_map/cond/branch_1_fun/down/pallas_call | solution.py:69
  189.6 5.0 %collective-permute-done.18.other_ref = bf16[512,384]{1,0:T(8,128)(2,1)S(1)} collective-permute-done((bf16[512,384]{1,0:T(8,128)(2,1)S(1)}, bf16[512,384]{1,0:T(8,128)(2,1)S(1)}, u32[]{:S(2)}, u32[]{:S(2)}) %collective-permute-start.18) | collective-permute-done | bytes 393248 | tf_op jit(solution)/shard_map/cond/branch_1_fun/ppermute | solution.py:95
  204.0 21.6 %collective-permute-done.17 = bf16[2,128,2048]{2,1,0:T(8,128)(2,1)S(1)} collective-permute-done((bf16[2,128,2048]{2,1,0:T(8,128)(2,1)S(1)}, bf16[2,128,2048]{2,1,0:T(8,128)(2,1)S(1)}, u32[]{:S(2)}, u32[]{:S(2)}) %collective-permute-start.17) | collective-permute-done | bytes 1048608 | tf_op jit(solution)/shard_map/cond/branch_1_fun/ppermute | solution.py:95
  226.9 19.9 %collective-permute-done.22 = bf16[2,128,2048]{2,1,0:T(8,128)(2,1)S(1)} collective-permute-done((bf16[2,128,2048]{2,1,0:T(8,128)(2,1)S(1)}, bf16[2,128,2048]{2,1,0:T(8,128)(2,1)S(1)}, u32[]{:S(2)}, u32[]{:S(2)}) %collective-permute-start.22) | collective-permute-done | bytes 1048608 | tf_op jit(solution)/shard_map/cond/branch_1_fun/ppermute | solution.py:95
  248.5 5.1 %collective-permute-done.34 = bf16[128,4096]{1,0:T(8,128)(2,1)} collective-permute-done((bf16[128,4096]{1,0:T(8,128)(2,1)}, bf16[128,4096]{1,0:T(8,128)(2,1)}, u32[]{:S(2)}, u32[]{:S(2)}) %collective-permute-start.34) | collective-permute-done | bytes 1048608 | tf_op jit(solution)/shard_map/ppermute | solution.py:95
  258.6 4.8 %maximum_select_fusion = bf16[1,384,4096]{2,1,0:T(8,128)(2,1)} fusion(bf16[1,128,4096]{2,1,0:T(8,128)(2,1)} %bitcast.50, bf16[1,256,4096]{2,1,0:T(8,128)(2,1)} %bitcast.49, pred[]{:T(512)S(6)} %eq.80, bf16[1,2,384,4096]{3,2,1,0:T(8,128)(2,1)} %param.18), kind=kLoop, calls=%fused_computation.24 | loop fusion | flops 7864320 | bytes 9437185 | tf_op jit(solution)/shard_map/jit(_where)/select_n | solution.py:248
  263.4 6.1 %collective-permute-done.36 = bf16[128,2048]{1,0:T(8,128)(2,1)S(1)} collective-permute-done((bf16[128,2048]{1,0:T(8,128)(2,1)S(1)}, bf16[128,2048]{1,0:T(8,128)(2,1)S(1)}, u32[]{:S(2)}, u32[]{:S(2)}) %collective-permute-start.36) | collective-permute-done | bytes 524320 | tf_op jit(solution)/shard_map/ppermute | solution.py:95
  270.8 2.9 bitcast_select_fusion.1
  273.7 13.0 %collective-permute-done.38 = bf16[128,2048]{1,0:T(8,128)(2,1)S(1)} collective-permute-done((bf16[128,2048]{1,0:T(8,128)(2,1)S(1)}, bf16[128,2048]{1,0:T(8,128)(2,1)S(1)}, u32[]{:S(2)}, u32[]{:S(2)}) %collective-permute-start.38) | collective-permute-done | bytes 524320 | tf_op jit(solution)/shard_map/ppermute | solution.py:95
  286.7 8.3 %collective-permute-done.37 = bf16[128,2048]{1,0:T(8,128)(2,1)S(1)} collective-permute-done((bf16[128,2048]{1,0:T(8,128)(2,1)S(1)}, bf16[128,2048]{1,0:T(8,128)(2,1)S(1)}, u32[]{:S(2)}, u32[]{:S(2)}) %collective-permute-start.37) | collective-permute-done | bytes 524320 | tf_op jit(solution)/shard_map/ppermute | solution.py:95
  295.8 103.4 %conditional.5 = ((bf16[384,4096]{1,0:T(8,128)(2,1)S(1)}, bf16[384,2048]{1,0:T(8,128)(2,1)})) conditional(s32[]{:T(128)} %convert_element_type.101, (bf16[384,4096]{1,0:T(8,128)(2,1)S(1)}, bf16[384,2048]{1,0:T(8,128)(2,1)}) %tuple.74, (bf16[384,4096]{1,0:T(8,128)(2,1)S(1)}, bf16[384,2048]{1,0:T(8,128)(2,1)}) %tuple.75), branch_computations={%region_12.13_spmd, %region_13.14_spmd} | conditional | bytes 28311656 | solution.py:243
  298.7 99.0 %collective-permute-done.1 = bf16[384,2048]{1,0:T(8,128)(2,1)S(1)} collective-permute-done((bf16[384,2048]{1,0:T(8,128)(2,1)}, bf16[384,2048]{1,0:T(8,128)(2,1)S(1)}, u32[]{:S(2)}, u32[]{:S(2)}) %collective-permute-start.1) | collective-permute-done | bytes 1572896 | tf_op jit(solution)/shard_map/cond/branch_1_fun/ppermute | solution.py:95
  401.7 3.2 fusion
  405.0 3.2 maximum_bitcast_fusion.4
  (184 shorter events, 90.2 us)
Async XLA Ops:
  0.6 26.3 %collective-permute-start.23 = (bf16[128,2048]{1,0:T(8,128)(2,1)}, bf16[128,2048]{1,0:T(8,128)(2,1)S(1)}, u32[]{:S(2)}, u32[]{:S(2)}) collective-permute-start(bf16[128,2048]{1,0:T(8,128)(2,1)} %param.13), channel_id=1, source_target_pairs={{0,8},{4,12},{8,0},{12,4},{1,9},{5,13},{9,1},{13,5},{2,10},{6,14},... | collective-permute-start | bytes 1572872 | tf_op jit(solution)/shard_map/ppermute | solution.py:95
  1.0 25.9 %collective-permute-start.24 = (bf16[128,2048]{1,0:T(8,128)(2,1)}, bf16[128,2048]{1,0:T(8,128)(2,1)S(1)}, u32[]{:S(2)}, u32[]{:S(2)}) collective-permute-start(bf16[128,2048]{1,0:T(8,128)(2,1)} %param.13), channel_id=1, source_target_pairs={{0,4},{4,0},{8,12},{12,8},{1,5},{5,1},{9,13},{13,9},{2,6},{6,2},{1... | collective-permute-start | bytes 1572872 | tf_op jit(solution)/shard_map/ppermute | solution.py:95
  1.2 25.7 %collective-permute-start.25 = (bf16[128,2048]{1,0:T(8,128)(2,1)}, bf16[128,2048]{1,0:T(8,128)(2,1)S(1)}, u32[]{:S(2)}, u32[]{:S(2)}) collective-permute-start(bf16[128,2048]{1,0:T(8,128)(2,1)} %param.13), channel_id=1, source_target_pairs={{0,16},{16,0},{1,17},{17,1},{2,18},{18,2},{3,19},{19,3},{4,20},{20... | collective-permute-start | bytes 1572872 | tf_op jit(solution)/shard_map/ppermute | solution.py:95
  3.0 24.8 %collective-permute-start.26 = (bf16[128,2048]{1,0:T(8,128)(2,1)}, bf16[128,2048]{1,0:T(8,128)(2,1)S(1)}, u32[]{:S(2)}, u32[]{:S(2)}) collective-permute-start(bf16[128,2048]{1,0:T(8,128)(2,1)} %param.13), channel_id=1, source_target_pairs={{0,2},{2,0},{1,3},{3,1},{4,6},{6,4},{5,7},{7,5},{8,10},{10,8},{9,1... | collective-permute-start | bytes 1572872 | tf_op jit(solution)/shard_map/ppermute | solution.py:95
  6.0 20.9 %collective-permute-start.27 = (f32[1,16,128]{2,1,0:T(8,128)S(1)}, f32[1,16,128]{2,1,0:T(8,128)S(1)}, u32[]{:S(2)}, u32[]{:S(2)}) collective-permute-start(f32[1,16,128]{2,1,0:T(8,128)S(1)} %select_bitcast_fusion), channel_id=1, source_target_pairs={{0,8},{4,12},{8,0},{12,4},{1,9},{5,13},{9,1},{13,5},{2,10},{6,14},... | collective-permute-start | bytes 24584 | tf_op jit(solution)/shard_map/ppermute | solution.py:95
  30.0 14.4 %collective-permute-start.28 = (bf16[128,2048]{1,0:T(8,128)(2,1)}, bf16[128,2048]{1,0:T(8,128)(2,1)S(1)}, u32[]{:S(2)}, u32[]{:S(2)}) collective-permute-start(bf16[128,2048]{1,0:T(8,128)(2,1)} %copy-done.12), channel_id=1, source_target_pairs={{0,4},{4,0},{8,12},{12,8},{1,5},{5,1},{9,13},{13,9},{2,6},{6,2},{1... | collective-permute-start | bytes 1572872 | tf_op jit(solution)/shard_map/ppermute | solution.py:95
  30.6 13.8 %collective-permute-start.29 = (bf16[128,2048]{1,0:T(8,128)(2,1)}, bf16[128,2048]{1,0:T(8,128)(2,1)S(1)}, u32[]{:S(2)}, u32[]{:S(2)}) collective-permute-start(bf16[128,2048]{1,0:T(8,128)(2,1)} %copy-done.12), channel_id=1, source_target_pairs={{0,16},{16,0},{1,17},{17,1},{2,18},{18,2},{3,19},{19,3},{4,20},{20... | collective-permute-start | bytes 1572872 | tf_op jit(solution)/shard_map/ppermute | solution.py:95
  32.1 13.2 %collective-permute-start.30 = (bf16[128,2048]{1,0:T(8,128)(2,1)}, bf16[128,2048]{1,0:T(8,128)(2,1)S(1)}, u32[]{:S(2)}, u32[]{:S(2)}) collective-permute-start(bf16[128,2048]{1,0:T(8,128)(2,1)} %copy-done.12), channel_id=1, source_target_pairs={{0,2},{2,0},{1,3},{3,1},{4,6},{6,4},{5,7},{7,5},{8,10},{10,8},{9,1... | collective-permute-start | bytes 1572872 | tf_op jit(solution)/shard_map/ppermute | solution.py:95
  46.9 92.0 %collective-permute-start.33 = (bf16[256,4096]{1,0:T(8,128)(2,1)}, bf16[256,4096]{1,0:T(8,128)(2,1)}, u32[]{:S(2)}, u32[]{:S(2)}) collective-permute-start(bf16[256,4096]{1,0:T(8,128)(2,1)} %slice.116), channel_id=1, source_target_pairs={{0,8},{4,12},{8,0},{12,4},{1,9},{5,13},{9,1},{13,5},{2,10},{6,14},... | collective-permute-start | bytes 6291464 | tf_op jit(solution)/shard_map/ppermute | solution.py:95
  49.7 14.9 %collective-permute-start.2 = (bf16[128,2048]{1,0:T(8,128)(2,1)S(1)}, bf16[128,2048]{1,0:T(8,128)(2,1)S(1)}, u32[]{:S(2)}, u32[]{:S(2)}) collective-permute-start(bf16[128,2048]{1,0:T(8,128)(2,1)S(1)} %get-tuple-element.46), channel_id=1, source_target_pairs={{0,16},{16,0},{1,17},{17,1},{2,18},{18,2},{3,19},{19,3},{4,20},{20... | collective-permute-start | bytes 1572872 | tf_op jit(solution)/shard_map/cond/branch_1_fun/ppermute | solution.py:95
  50.2 14.4 %collective-permute-start.3 = (bf16[128,2048]{1,0:T(8,128)(2,1)S(1)}, bf16[128,2048]{1,0:T(8,128)(2,1)S(1)}, u32[]{:S(2)}, u32[]{:S(2)}) collective-permute-start(bf16[128,2048]{1,0:T(8,128)(2,1)S(1)} %get-tuple-element.46), channel_id=1, source_target_pairs={{0,2},{2,0},{1,3},{3,1},{4,6},{6,4},{5,7},{7,5},{8,10},{10,8},{9,1... | collective-permute-start | bytes 1572872 | tf_op jit(solution)/shard_map/cond/branch_1_fun/ppermute | solution.py:95
  51.8 21.0 %collective-permute-start.4 = (bf16[128,2048]{1,0:T(8,128)(2,1)S(1)}, bf16[128,2048]{1,0:T(8,128)(2,1)S(1)}, u32[]{:S(2)}, u32[]{:S(2)}) collective-permute-start(bf16[128,2048]{1,0:T(8,128)(2,1)S(1)} %get-tuple-element.47), channel_id=1, source_target_pairs={{0,16},{16,0},{1,17},{17,1},{2,18},{18,2},{3,19},{19,3},{4,20},{20... | collective-permute-start | bytes 1572872 | tf_op jit(solution)/shard_map/cond/branch_1_fun/ppermute | solution.py:95
  74.2 14.9 %collective-permute-start.8 = (bf16[128,2048]{1,0:T(8,128)(2,1)S(1)}, bf16[128,2048]{1,0:T(8,128)(2,1)S(1)}, u32[]{:S(2)}, u32[]{:S(2)}) collective-permute-start(bf16[128,2048]{1,0:T(8,128)(2,1)S(1)} %get-tuple-element.50), channel_id=1, source_target_pairs={{0,2},{2,0},{1,3},{3,1},{4,6},{6,4},{5,7},{7,5},{8,10},{10,8},{9,1... | collective-permute-start | bytes 1572872 | tf_op jit(solution)/shard_map/cond/branch_1_fun/ppermute | solution.py:95
  75.7 21.2 %collective-permute-start.6 = (bf16[128,2048]{1,0:T(8,128)(2,1)S(1)}, bf16[128,2048]{1,0:T(8,128)(2,1)S(1)}, u32[]{:S(2)}, u32[]{:S(2)}) collective-permute-start(bf16[128,2048]{1,0:T(8,128)(2,1)S(1)} %collective-permute-done.2), channel_id=1, source_target_pairs={{0,2},{2,0},{1,3},{3,1},{4,6},{6,4},{5,7},{7,5},{8,10},{10,8},{9,1... | collective-permute-start | bytes 1572872 | tf_op jit(solution)/shard_map/cond/branch_1_fun/ppermute | solution.py:95
  99.8 17.0 %collective-permute-start.13 = (bf16[384,2048]{1,0:T(8,128)(2,1)}, bf16[384,2048]{1,0:T(8,128)(2,1)}, u32[]{:S(2)}, u32[]{:S(2)}) collective-permute-start(bf16[384,2048]{1,0:T(8,128)(2,1)} %get-tuple-element.66), channel_id=1, source_target_pairs={{0,1},{1,0},{2,3},{3,2},{4,5},{5,4},{6,7},{7,6},{8,9},{9,8},{10,11... | collective-permute-start | bytes 4718600 | tf_op jit(solution)/shard_map/cond/branch_1_fun/ppermute | solution.py:95
  100.4 16.4 %collective-permute-start.10 = (bf16[128,2048]{1,0:T(8,128)(2,1)}, bf16[128,2048]{1,0:T(8,128)(2,1)}, u32[]{:S(2)}, u32[]{:S(2)}) collective-permute-start(bf16[128,2048]{1,0:T(8,128)(2,1)} %get-tuple-element.57), channel_id=1, source_target_pairs={{0,2},{2,0},{1,3},{3,1},{4,6},{6,4},{5,7},{7,5},{8,10},{10,8},{9,1... | collective-permute-start | bytes 1572872 | tf_op jit(solution)/shard_map/cond/branch_1_fun/ppermute | solution.py:95
  101.9 14.9 %collective-permute-start.11 = (bf16[128,2048]{1,0:T(8,128)(2,1)}, bf16[128,2048]{1,0:T(8,128)(2,1)}, u32[]{:S(2)}, u32[]{:S(2)}) collective-permute-start(bf16[128,2048]{1,0:T(8,128)(2,1)} %copy-done.25), channel_id=1, source_target_pairs={{0,16},{16,0},{1,17},{17,1},{2,18},{18,2},{3,19},{19,3},{4,20},{20... | collective-permute-start | bytes 1572872 | tf_op jit(solution)/shard_map/cond/branch_1_fun/ppermute | solution.py:95
  138.9 114.7 %collective-permute-start.35 = (bf16[384,2048]{1,0:T(8,128)(2,1)}, bf16[384,2048]{1,0:T(8,128)(2,1)}, u32[]{:S(2)}, u32[]{:S(2)}) collective-permute-start(bf16[384,2048]{1,0:T(8,128)(2,1)} %bitcast_select_fusion.2), channel_id=1, source_target_pairs={{0,8},{4,12},{8,0},{12,4},{1,9},{5,13},{9,1},{13,5},{2,10},{6,14},... | collective-permute-start | bytes 4718600 | tf_op jit(solution)/shard_map/ppermute | solution.py:95
  138.9 114.7 %collective-permute-start.34 = (bf16[128,4096]{1,0:T(8,128)(2,1)}, bf16[128,4096]{1,0:T(8,128)(2,1)}, u32[]{:S(2)}, u32[]{:S(2)}) collective-permute-start(bf16[128,4096]{1,0:T(8,128)(2,1)} %slice.117), channel_id=1, source_target_pairs={{0,8},{4,12},{8,0},{12,4},{1,9},{5,13},{9,1},{13,5},{2,10},{6,14},... | collective-permute-start | bytes 3145736 | tf_op jit(solution)/shard_map/ppermute | solution.py:95
  143.9 16.5 %collective-permute-start.19 = (bf16[2,4,128,2048]{3,2,1,0:T(8,128)(2,1)}, bf16[2,4,128,2048]{3,2,1,0:T(8,128)(2,1)}, u32[]{:S(2)}, u32[]{:S(2)}) collective-permute-start(bf16[2,4,128,2048]{3,2,1,0:T(8,128)(2,1)} %get-tuple-element.78.x_ref), channel_id=1, source_target_pairs={{0,1},{1,0},{2,3},{3,2},{4,5},{5,4},{6,7},{7,6},{8,9},{9,8},{10,11... | collective-permute-start | bytes 12582920 | tf_op jit(solution)/shard_map/cond/branch_1_fun/ppermute | solution.py:95
  160.3 36.8 %collective-permute-start.16 = (bf16[512,2048]{1,0:T(8,128)(2,1)S(1)}, bf16[512,2048]{1,0:T(8,128)(2,1)}, u32[]{:S(2)}, u32[]{:S(2)}) collective-permute-start(bf16[512,2048]{1,0:T(8,128)(2,1)S(1)} %down.5), channel_id=1, source_target_pairs={{0,1},{1,0},{2,3},{3,2},{4,5},{5,4},{6,7},{7,6},{8,9},{9,8},{10,11... | collective-permute-start | bytes 6291464 | tf_op jit(solution)/shard_map/cond/branch_1_fun/ppermute | solution.py:95
  183.1 18.0 %collective-permute-start.21 = (bf16[512,2048]{1,0:T(8,128)(2,1)}, bf16[512,2048]{1,0:T(8,128)(2,1)}, u32[]{:S(2)}, u32[]{:S(2)}) collective-permute-start(bf16[512,2048]{1,0:T(8,128)(2,1)} %down.7), channel_id=1, source_target_pairs={{0,1},{1,0},{2,3},{3,2},{4,5},{5,4},{6,7},{7,6},{8,9},{9,8},{10,11... | collective-permute-start | bytes 6291464 | tf_op jit(solution)/shard_map/cond/branch_1_fun/ppermute | solution.py:95
  199.5 26.1 %collective-permute-start.17 = (bf16[2,128,2048]{2,1,0:T(8,128)(2,1)S(1)}, bf16[2,128,2048]{2,1,0:T(8,128)(2,1)S(1)}, u32[]{:S(2)}, u32[]{:S(2)}) collective-permute-start(bf16[2,128,2048]{2,1,0:T(8,128)(2,1)S(1)} %bitcast.97), channel_id=1, source_target_pairs={{0,2},{2,0},{1,3},{3,1},{4,6},{6,4},{5,7},{7,5},{8,10},{10,8},{9,1... | collective-permute-start | bytes 3145736 | tf_op jit(solution)/shard_map/cond/branch_1_fun/ppermute | solution.py:95
  203.4 43.4 %collective-permute-start.22 = (bf16[2,128,2048]{2,1,0:T(8,128)(2,1)S(1)}, bf16[2,128,2048]{2,1,0:T(8,128)(2,1)S(1)}, u32[]{:S(2)}, u32[]{:S(2)}) collective-permute-start(bf16[2,128,2048]{2,1,0:T(8,128)(2,1)S(1)} %bitcast.98), channel_id=1, source_target_pairs={{0,2},{2,0},{1,3},{3,1},{4,6},{6,4},{5,7},{7,5},{8,10},{10,8},{9,1... | collective-permute-start | bytes 3145736 | tf_op jit(solution)/shard_map/cond/branch_1_fun/ppermute | solution.py:95
  248.5 153.2 %collective-permute-start.39 = (bf16[256,4096]{1,0:T(8,128)(2,1)}, bf16[256,4096]{1,0:T(8,128)(2,1)}, u32[]{:S(2)}, u32[]{:S(2)}) collective-permute-start(bf16[256,4096]{1,0:T(8,128)(2,1)} %collective-permute-done.33), channel_id=1, source_target_pairs={{0,1},{1,0},{2,3},{3,2},{4,5},{5,4},{6,7},{7,6},{8,9},{9,8},{10,11... | collective-permute-start | bytes 6291464 | tf_op jit(solution)/shard_map/ppermute | solution.py:95
  254.7 14.8 %collective-permute-start.36 = (bf16[128,2048]{1,0:T(8,128)(2,1)S(1)}, bf16[128,2048]{1,0:T(8,128)(2,1)S(1)}, u32[]{:S(2)}, u32[]{:S(2)}) collective-permute-start(bf16[128,2048]{1,0:T(8,128)(2,1)S(1)} %slice_bitcast_fusion.6), channel_id=1, source_target_pairs={{0,4},{4,0},{8,12},{12,8},{1,5},{5,1},{9,13},{13,9},{2,6},{6,2},{1... | collective-permute-start | bytes 1572872 | tf_op jit(solution)/shard_map/ppermute | solution.py:95
  256.0 30.7 %collective-permute-start.38 = (bf16[128,2048]{1,0:T(8,128)(2,1)S(1)}, bf16[128,2048]{1,0:T(8,128)(2,1)S(1)}, u32[]{:S(2)}, u32[]{:S(2)}) collective-permute-start(bf16[128,2048]{1,0:T(8,128)(2,1)S(1)} %fusion.4), channel_id=1, source_target_pairs={{0,4},{4,0},{8,12},{12,8},{1,5},{5,1},{9,13},{13,9},{2,6},{6,2},{1... | collective-permute-start | bytes 1572872 | tf_op jit(solution)/shard_map/ppermute | solution.py:95
  258.1 150.1 %collective-permute-start.41 = (bf16[384,2048]{1,0:T(8,128)(2,1)}, bf16[384,2048]{1,0:T(8,128)(2,1)}, u32[]{:S(2)}, u32[]{:S(2)}) collective-permute-start(bf16[384,2048]{1,0:T(8,128)(2,1)} %collective-permute-done.35), channel_id=1, source_target_pairs={{0,1},{1,0},{2,3},{3,2},{4,5},{5,4},{6,7},{7,6},{8,9},{9,8},{10,11... | collective-permute-start | bytes 4718600 | tf_op jit(solution)/shard_map/ppermute | solution.py:95
  258.1 143.6 %collective-permute-start.40 = (bf16[128,4096]{1,0:T(8,128)(2,1)}, bf16[128,4096]{1,0:T(8,128)(2,1)}, u32[]{:S(2)}, u32[]{:S(2)}) collective-permute-start(bf16[128,4096]{1,0:T(8,128)(2,1)} %collective-permute-done.34), channel_id=1, source_target_pairs={{0,1},{1,0},{2,3},{3,2},{4,5},{5,4},{6,7},{7,6},{8,9},{9,8},{10,11... | collective-permute-start | bytes 3145736 | tf_op jit(solution)/shard_map/ppermute | solution.py:95
  270.7 24.3 %collective-permute-start.37 = (bf16[128,2048]{1,0:T(8,128)(2,1)S(1)}, bf16[128,2048]{1,0:T(8,128)(2,1)S(1)}, u32[]{:S(2)}, u32[]{:S(2)}) collective-permute-start(bf16[128,2048]{1,0:T(8,128)(2,1)S(1)} %fusion.1), channel_id=1, source_target_pairs={{0,8},{4,12},{8,0},{12,4},{1,9},{5,13},{9,1},{13,5},{2,10},{6,14},... | collective-permute-start | bytes 1572872 | tf_op jit(solution)/shard_map/ppermute | solution.py:95
  295.8 103.2 %collective-permute-start = (bf16[384,4096]{1,0:T(8,128)(2,1)S(1)}, bf16[384,4096]{1,0:T(8,128)(2,1)S(1)}, u32[]{:S(2)}, u32[]{:S(2)}) collective-permute-start(bf16[384,4096]{1,0:T(8,128)(2,1)S(1)} %get-tuple-element.82), channel_id=1, source_target_pairs={{0,8},{4,12},{8,0},{12,4},{1,9},{5,13},{9,1},{13,5},{2,10},{6,14},... | collective-permute-start | bytes 9437192 | tf_op jit(solution)/shard_map/cond/branch_1_fun/ppermute | solution.py:95
  295.8 102.0 %collective-permute-start.1 = (bf16[384,2048]{1,0:T(8,128)(2,1)}, bf16[384,2048]{1,0:T(8,128)(2,1)S(1)}, u32[]{:S(2)}, u32[]{:S(2)}) collective-permute-start(bf16[384,2048]{1,0:T(8,128)(2,1)} %get-tuple-element.83), channel_id=1, source_target_pairs={{0,8},{4,12},{8,0},{12,4},{1,9},{5,13},{9,1},{13,5},{2,10},{6,14},... | collective-permute-start | bytes 4718600 | tf_op jit(solution)/shard_map/cond/branch_1_fun/ppermute | solution.py:95
  (44 other events, 430.4 us)
where the time goes:
time: 413 us; the launch traced here: 412 us
  waiting for transfers between devices  268 us (65%)
  Pallas kernels  44.7 us (11%)
  other arithmetic  43.8 us (11%)
  starting transfers between devices  38.6 us (9%)
  local copies, waits for them, and re-layouts  14.9 us (4%)
    ppermute x42, waiting for transfers between devices, hop(): lax.ppermute(value, axis, [(p, p ^ mask) for p in range(lax.axis_size(axi...  268 us
    ppermute x42, starting transfers between devices, hop(): lax.ppermute(value, axis, [(p, p ^ mask) for p in range(lax.axis_size(axi...  38.6 us
    pallas_call x4, Pallas kernels, project(): pl.pallas_call(project_kernel, grid_spec=pltpu.PrefetchScalarGridSpec(num...  27.2 us
    pallas_call x4, Pallas kernels, down(): pl.pallas_call(down_kernel, grid_spec=pltpu.PrefetchScalarGridSpec(num_sc...  17.5 us
  transfers between devices with their start and end apart: 42, of which 22 were waited for; matrix products, arithmetic and copies ran while one was open for 12% of the time, Pallas kernels for 11%

commit v1 on v0

--- a/solution.py
+++ b/solution.py
@@ -161,8 +161,10 @@
     line, line_y = across_y(*late)
     line = (line + wide(line_y)).astype(jnp.bfloat16)
     early = serve(early_own, early_own_cross, early_other, early_other_cross, w_down, scale[:, 0])
+    line = (wide(line[0]) + wide(hop(line[1], "z", 1))).astype(jnp.bfloat16)
     total, total_y = across_y(*early)
-    return line, total + wide(total_y)
+    total = total + wide(total_y)
+    return line, total[0], total[1].astype(jnp.bfloat16)
 
 
 def guarded(valid, stage, *operands):
@@ -228,13 +230,14 @@
     )
     arrived_second, arrived_down = hop(lane_second, "z", 2), hop(lane_down, "z", 2)
     handed_first = hop(arrived_first, "core")
-    line, total = guarded(valid, expert_stage, *staged, w_pair, w_down)
-    line, total, arrived_second, arrived_down = tie(line, total, arrived_second, arrived_down)
-    line = (wide(line[0]) + wide(hop(line[1], "z", 1))).astype(jnp.bfloat16)
-    closing = hop(total[1].astype(jnp.bfloat16), "z", 1)
-    over, closing, *last = tie(hop(line, "z", 2), closing, *tails)
-    handed_down, handed_second = hop(arrived_down, "core"), hop(arrived_second, "core")
-    moe_out = (total[0] + wide(closing) + wide(over)).astype(jnp.bfloat16)
+    line, total, leave = guarded(valid, expert_stage, *staged, w_pair, w_down)
+    line, total, leave, arrived_second, arrived_down = tie(
+        line, total, leave, arrived_second, arrived_down
+    )
+    over, closing = hop(line, "z", 2), hop(leave, "z", 1)
+    handed_first, handed_second, handed_down, *last = tie(
+        handed_first, hop(arrived_second, "core"), hop(arrived_down, "core"), *tails
+    )
     partner = (slots + half * jnp.tile(swap_flag, 2)) % ncol
     column_load = jnp.sum(
         jnp.where(partner[:, None] == slots[None, :], counts[None, :], 0.0), axis=1
@@ -249,6 +252,8 @@
     tails = [jnp.where(alone, new, old) for new, old in zip(handed, rest)]
     slot_gate_up = jnp.stack([heads[0], tails[0]])[None]
     slot_down = jnp.concatenate([heads[1], tails[1]])[None]
+    over, closing, slot_gate_up, slot_down = tie(over, closing, slot_gate_up, slot_down)
+    moe_out = (total + wide(closing) + wide(over)).astype(jnp.bfloat16)
     return (moe_out, column_load, slot_gate_up, slot_down)
 
 

time: 413 us -> 302 us (0.73)
  waiting for transfers between devices: 268 us -> 154 us
    ppermute x42 -> x40, waiting for transfers between devices: 268 us -> 154 us  [hop(): lax.ppermute(value, axis, [(p, p ^ mask) for p in range(lax.axis_size(axi...]
    ppermute x42 -> x40, starting transfers between devices: 38.6 us -> 36.4 us  [hop(): lax.ppermute(value, axis, [(p, p ^ mask) for p in range(lax.axis_size(axi...]
  transfers between devices with their start and end apart: 42 -> 40, of which waited for: 22 -> 18; matrix products, arithmetic and copies ran while one was open for 12% -> 16% of each run, Pallas kernels for 11% -> 15%
where the time goes in v1:
time: 302 us; the launch traced here: 297 us
  waiting for transfers between devices  154 us (51%)
  Pallas kernels  44.6 us (15%)
  other arithmetic  43.6 us (14%)
  starting transfers between devices  36.4 us (12%)
  local copies, waits for them, and re-layouts  16.3 us (5%)
    ppermute x40, waiting for transfers between devices, hop(): lax.ppermute(value, axis, [(p, p ^ mask) for p in range(lax.axis_size(axi...  154 us
    ppermute x40, starting transfers between devices, hop(): lax.ppermute(value, axis, [(p, p ^ mask) for p in range(lax.axis_size(axi...  36.4 us
    pallas_call x4, Pallas kernels, project(): pl.pallas_call(project_kernel, grid_spec=pltpu.PrefetchScalarGridSpec(num...  27.3 us
    pallas_call x4, Pallas kernels, down(): pl.pallas_call(down_kernel, grid_spec=pltpu.PrefetchScalarGridSpec(num_sc...  17.3 us
    select_n x2, other arithmetic, body(): heads = [jnp.where(own, new, old) for new, old in zip(arrived, heads)]  7.53 us
    convert_element_type x2, other arithmetic, across_y(): leave = (wide(kept[1]) + wide(received[1])).astype(jnp.bfloat16)  6.35 us
    unnamed x40, local copies, waits for them, and re-layouts  6.11 us
  transfers between devices with their start and end apart: 40, of which 18 were waited for; matrix products, arithmetic and copies ran while one was open for 16% of the time, Pallas kernels for 15%

profile of v1, /device:TPU:24, one launch (start us, length us, event | category | flops | bytes accessed | tf_op | source)
XLA Modules:
  0.0 297.5 jit_solution(11703247017558310845)
XLA Ops:
  6.0 2.7 collective-permute-start.28
  10.8 16.1 %collective-permute-done.28 = f32[1,16,128]{2,1,0:T(8,128)S(1)} collective-permute-done((f32[1,16,128]{2,1,0:T(8,128)S(1)}, f32[1,16,128]{2,1,0:T(8,128)S(1)}, u32[]{:S(2)}, u32[]{:S(2)}) %collective-permute-start.28) | collective-permute-done | bytes 8224 | tf_op jit(solution)/shard_map/ppermute | solution.py:95
  35.2 3.2 %bitcast_select_fusion = bf16[384,4096]{1,0:T(8,128)(2,1)S(1)} fusion(bf16[384,4096]{1,0:T(8,128)(2,1)} %collective-permute-done.33, pred[]{:T(512)S(6)} %eq.80, bf16[1,2,384,4096]{3,2,1,0:T(8,128)(2,1)} %param.18), kind=kLoop, calls=%fused_computation.35 | loop fusion | flops 1572864 | bytes 9437185 | tf_op jit(solution)/shard_map/jit(_where)/select_n | solution.py:212
  38.4 6.1 %collective-permute-done.32 = f32[2,16,128]{2,1,0:T(8,128)S(1)} collective-permute-done((f32[2,16,128]{2,1,0:T(8,128)S(1)}, f32[2,16,128]{2,1,0:T(8,128)S(1)}, u32[]{:S(2)}, u32[]{:S(2)}) %collective-permute-start.32) | collective-permute-done | bytes 16416 | tf_op jit(solution)/shard_map/ppermute | solution.py:95
  49.6 77.9 %conditional.3 = (bf16[2,4,128,2048]{3,2,1,0:T(8,128)(2,1)}, bf16[512,384]{1,0:T(8,128)(2,1)S(1)}, bf16[512,384]{1,0:T(8,128)(2,1)}, bf16[512,384]{1,0:T(8,128)(...) conditional(s32[]{:T(128)} %bitcast.41, () %tuple.42, ...), branch_computations={%region_4.5_spmd, %region_5.8_spmd} | conditional | flops 6459439104 | bytes 133833904 | solution.py:173
  53.8 9.5 %collective-permute-done.5 = f32[4,16,128]{2,1,0:T(8,128)S(1)} collective-permute-done((f32[4,16,128]{2,1,0:T(8,128)S(1)}, f32[4,16,128]{2,1,0:T(8,128)S(1)}, u32[]{:S(2)}, u32[]{:S(2)}) %collective-permute-start.5) | collective-permute-done | bytes 32800 | tf_op jit(solution)/shard_map/cond/branch_1_fun/ppermute | solution.py:95
  64.6 8.2 %collective-permute-done.4 = bf16[128,2048]{1,0:T(8,128)(2,1)S(1)} collective-permute-done((bf16[128,2048]{1,0:T(8,128)(2,1)S(1)}, bf16[128,2048]{1,0:T(8,128)(2,1)S(1)}, u32[]{:S(2)}, u32[]{:S(2)}) %collective-permute-start.4) | collective-permute-done | bytes 524320 | tf_op jit(solution)/shard_map/cond/branch_1_fun/ppermute | solution.py:95
  77.4 6.7 %collective-permute-done.7 = bf16[128,2048]{1,0:T(8,128)(2,1)S(1)} collective-permute-done((bf16[128,2048]{1,0:T(8,128)(2,1)S(1)}, bf16[128,2048]{1,0:T(8,128)(2,1)S(1)}, u32[]{:S(2)}, u32[]{:S(2)}) %collective-permute-start.7) | collective-permute-done | bytes 524320 | tf_op jit(solution)/shard_map/cond/branch_1_fun/ppermute | solution.py:95
  84.1 4.8 %collective-permute-done.8 = bf16[128,2048]{1,0:T(8,128)(2,1)S(1)} collective-permute-done((bf16[128,2048]{1,0:T(8,128)(2,1)S(1)}, bf16[128,2048]{1,0:T(8,128)(2,1)S(1)}, u32[]{:S(2)}, u32[]{:S(2)}) %collective-permute-start.8) | collective-permute-done | bytes 524320 | tf_op jit(solution)/shard_map/cond/branch_1_fun/ppermute | solution.py:95
  89.0 7.9 %collective-permute-done.6 = bf16[128,2048]{1,0:T(8,128)(2,1)S(1)} collective-permute-done((bf16[128,2048]{1,0:T(8,128)(2,1)S(1)}, bf16[128,2048]{1,0:T(8,128)(2,1)S(1)}, u32[]{:S(2)}, u32[]{:S(2)}) %collective-permute-start.6) | collective-permute-done | bytes 524320 | tf_op jit(solution)/shard_map/cond/branch_1_fun/ppermute | solution.py:95
  102.4 7.6 %project.4 = bf16[512,384]{1,0:T(8,128)(2,1)S(1)} custom-call(s32[1]{0:T(128)} %bitcast.7.part_ref, bf16[2,4,128,2048]{3,2,1,0:T(8,128)(2,1)} %pad_maximum_fusion.x_ref, bf16[768,4096]{1,0:T(8,128)(2,1)} %get-tuple-element.64.own_w_ref.other_w_ref, bf16[768,4096]{1,0:T(8,128)(2,1)} %get-tuple-element.64.own_w_ref.other_w_ref), custom_call_target="tpu_custom_call" | custom-call | flops 3221225472 | bytes 10485760 | tf_op jit(solution)/shard_map/cond/branch_1_fun/project/pallas_call | solution.py:36
  110.4 6.4 %project.5 = bf16[512,384]{1,0:T(8,128)(2,1)} custom-call(s32[1]{0:T(128)} %bitcast.7.part_ref, bf16[2,4,128,2048]{3,2,1,0:T(8,128)(2,1)} %collective-permute-done.12.x_ref, bf16[768,4096]{1,0:T(8,128)(2,1)S(1)} %bitcast.84, bf16[768,4096]{1,0:T(8,128)(2,1)S(1)} %bitcast.84), custom_call_target="tpu_custom_call" | custom-call | flops 3221225472 | bytes 10485760 | tf_op jit(solution)/shard_map/cond/branch_1_fun/project/pallas_call | solution.py:36
  122.8 4.7 %collective-permute-done.14 = bf16[512,384]{1,0:T(8,128)(2,1)} collective-permute-done((bf16[512,384]{1,0:T(8,128)(2,1)S(1)}, bf16[512,384]{1,0:T(8,128)(2,1)}, u32[]{:S(2)}, u32[]{:S(2)}) %collective-permute-start.14) | collective-permute-done | bytes 393248 | tf_op jit(solution)/shard_map/cond/branch_1_fun/ppermute | solution.py:95
  127.5 2.8 bitcast_select_fusion.2
  130.2 8.6 %collective-permute-done.34 = bf16[256,4096]{1,0:T(8,128)(2,1)} collective-permute-done((bf16[256,4096]{1,0:T(8,128)(2,1)}, bf16[256,4096]{1,0:T(8,128)(2,1)}, u32[]{:S(2)}, u32[]{:S(2)}) %collective-permute-start.34) | collective-permute-done | bytes 2097184 | tf_op jit(solution)/shard_map/ppermute | solution.py:95
  138.9 2.9 collective-permute-start.35
  142.6 125.3 %conditional.4 = (bf16[128,2048]{1,0:T(8,128)(2,1)}, f32[128,2048]{1,0:T(8,128)}, bf16[128,2048]{1,0:T(8,128)(2,1)}) conditional(s32[]{:T(128)} %bitcast.41, () %tuple.41, (bf16[1,768,2048]{2,1,0:T(8,128)(2,1)S(1)}, f32[2,2,512,1]{2,1,0,3:T(2,128)S(1)}, bf16[512,384]{1,0:T(8,128)(2,1)S(1)}, bf16[512,384]{1,0:T(8,128)(2,1)}, ...), branch_computations={%region_8.9_spmd, %region_9.10_spmd} | conditional | flops 12895911936 | bytes 185647680 | solution.py:173
  145.7 7.5 %project.6.own_ref = bf16[512,384]{1,0:T(8,128)(2,1)S(1)} custom-call(s32[1]{0:T(128)} %bitcast.26.part_ref, bf16[2,4,128,2048]{3,2,1,0:T(8,128)(2,1)} %get-tuple-element.78.x_ref, bf16[768,4096]{1,0:T(8,128)(2,1)} %get-tuple-element.79.own_w_ref.other_w_ref, bf16[768,4096]{1,0:T(8,128)(2,1)} %get-tuple-element.79.own_w_ref.other_w_ref), custom_call_target="tpu_custom_call" | custom-call | flops 3221225472 | bytes 10485760 | tf_op jit(solution)/shard_map/cond/branch_1_fun/project/pallas_call | solution.py:36
  154.5 5.7 %down.5 = bf16[512,2048]{1,0:T(8,128)(2,1)} custom-call(s32[1]{0:T(128)} %bitcast.26.part_ref, bf16[512,384]{1,0:T(8,128)(2,1)} %get-tuple-element.80.own_ref, bf16[512,384]{1,0:T(8,128)(2,1)S(1)} %collective-permute-done.15.other_ref, bf16[768,2048]{1,0:T(8,128)(2,1)} %bitcast.85, bf16[768,2048]{1,0:T(8,128)(2,1)} %bitcast.86, f32[512,1]{1,0:T(8,128)S(1)} %copy.22.scale_ref), custom_call_target="tpu_custom_call" | custom-call | flops 1610612736 | bytes 6029312 | tf_op jit(solution)/shard_map/cond/branch_1_fun/down/pallas_call | solution.py:69
  160.2 5.7 %project.7.own_ref = bf16[512,384]{1,0:T(8,128)(2,1)S(1)} custom-call(s32[1]{0:T(128)} %bitcast.26.part_ref, bf16[2,4,128,2048]{3,2,1,0:T(8,128)(2,1)} %collective-permute-done.20.x_ref, bf16[768,4096]{1,0:T(8,128)(2,1)S(1)} %copy-done, bf16[768,4096]{1,0:T(8,128)(2,1)S(1)} %copy-done), custom_call_target="tpu_custom_call" | custom-call | flops 3221225472 | bytes 10485760 | tf_op jit(solution)/shard_map/cond/branch_1_fun/project/pallas_call | solution.py:36
  167.7 4.7 %down.4 = bf16[512,2048]{1,0:T(8,128)(2,1)S(1)} custom-call(s32[1]{0:T(128)} %bitcast.26.part_ref, bf16[512,384]{1,0:T(8,128)(2,1)S(1)} %copy-done.14, bf16[512,384]{1,0:T(8,128)(2,1)} %get-tuple-element.74.other_ref, bf16[768,2048]{1,0:T(8,128)(2,1)} %bitcast.87, bf16[768,2048]{1,0:T(8,128)(2,1)} %bitcast.88, f32[512,1]{1,0:T(8,128)S(1)} %copy.21.scale_ref), custom_call_target="tpu_custom_call" | custom-call | flops 1610612736 | bytes 6029312 | tf_op jit(solution)/shard_map/cond/branch_1_fun/down/pallas_call | solution.py:69
  172.4 5.1 %collective-permute-done.21.other_ref = bf16[512,384]{1,0:T(8,128)(2,1)S(1)} collective-permute-done((bf16[512,384]{1,0:T(8,128)(2,1)S(1)}, bf16[512,384]{1,0:T(8,128)(2,1)S(1)}, u32[]{:S(2)}, u32[]{:S(2)}) %collective-permute-start.21) | collective-permute-done | bytes 393248 | tf_op jit(solution)/shard_map/cond/branch_1_fun/ppermute | solution.py:95
  177.5 2.5 down.7
  180.1 4.0 %add_convert_fusion.2 = (bf16[256,2048]{1,0:T(8,128)(2,1)}, f32[256,2048]{1,0:T(8,128)}) fusion(bf16[512,2048]{1,0:T(8,128)(2,1)} %collective-permute-done.16, bf16[512,2048]{1,0:T(8,128)(2,1)S(1)} %down.4), kind=kLoop, calls=%fused_computation.17 | loop fusion | flops 3670016 | bytes 7340032 | tf_op jit(solution)/shard_map/cond/branch_1_fun/convert_element_type | solution.py:117
  187.2 9.7 %collective-permute-done.19.other_ref = bf16[512,384]{1,0:T(8,128)(2,1)S(1)} collective-permute-done((bf16[512,384]{1,0:T(8,128)(2,1)S(1)}, bf16[512,384]{1,0:T(8,128)(2,1)S(1)}, u32[]{:S(2)}, u32[]{:S(2)}) %collective-permute-start.19) | collective-permute-done | bytes 393248 | tf_op jit(solution)/shard_map/cond/branch_1_fun/ppermute | solution.py:95
  196.9 4.4 %down.6 = bf16[512,2048]{1,0:T(8,128)(2,1)S(1)} custom-call(s32[1]{0:T(128)} %bitcast.26.part_ref, bf16[512,384]{1,0:T(8,128)(2,1)S(1)} %project.6.own_ref, bf16[512,384]{1,0:T(8,128)(2,1)S(1)} %collective-permute-done.19.other_ref, bf16[768,2048]{1,0:T(8,128)(2,1)} %bitcast.89, bf16[768,2048]{1,0:T(8,128)(2,1)} %bitcast.90, f32[512,1]{1,0:T(8,128)S(1)} %copy.23.scale_ref), custom_call_target="tpu_custom_call" | custom-call | flops 1610612736 | bytes 6029312 | tf_op jit(solution)/shard_map/cond/branch_1_fun/down/pallas_call | solution.py:69
  201.3 8.7 %collective-permute-done.17 = bf16[2,128,2048]{2,1,0:T(8,128)(2,1)} collective-permute-done((bf16[2,128,2048]{2,1,0:T(8,128)(2,1)}, bf16[2,128,2048]{2,1,0:T(8,128)(2,1)}, u32[]{:S(2)}, u32[]{:S(2)}) %collective-permute-start.17) | collective-permute-done | bytes 1048608 | tf_op jit(solution)/shard_map/cond/branch_1_fun/ppermute | solution.py:95
  215.6 49.1 %collective-permute-done.18 = bf16[128,2048]{1,0:T(8,128)(2,1)S(1)} collective-permute-done((bf16[128,2048]{1,0:T(8,128)(2,1)S(1)}, bf16[128,2048]{1,0:T(8,128)(2,1)S(1)}, u32[]{:S(2)}, u32[]{:S(2)}) %collective-permute-start.18) | collective-permute-done | bytes 524320 | tf_op jit(solution)/shard_map/cond/branch_1_fun/ppermute | solution.py:95
  271.0 2.7 bitcast_select_fusion.1
  273.7 4.8 %maximum_select_fusion = bf16[1,384,4096]{2,1,0:T(8,128)(2,1)} fusion(bf16[1,128,4096]{2,1,0:T(8,128)(2,1)} %bitcast.51, bf16[1,256,4096]{2,1,0:T(8,128)(2,1)} %bitcast.50, pred[]{:T(512)S(6)} %eq.80, bf16[1,2,384,4096]{3,2,1,0:T(8,128)(2,1)} %param.18), kind=kLoop, calls=%fused_computation.31 | loop fusion | flops 7864320 | bytes 9437185 | tf_op jit(solution)/shard_map/jit(_where)/select_n | solution.py:251
  287.8 3.2 %maximum_bitcast_fusion.4 = bf16[1,2,384,4096]{3,2,1,0:T(8,128)(2,1)} fusion(bf16[1,384,4096]{2,1,0:T(8,128)(2,1)S(1)} %fusion.2, bf16[1,384,4096]{2,1,0:T(8,128)(2,1)S(1)} %copy-done.6), kind=kLoop, calls=%fused_computation.30 | loop fusion | flops 3145728 | bytes 12582912 | tf_op jit(solution)/shard_map/broadcast_in_dim | solution.py:253
  291.0 3.9 %collective-permute-done.37 = bf16[128,2048]{1,0:T(8,128)(2,1)} collective-permute-done((bf16[128,2048]{1,0:T(8,128)(2,1)}, bf16[128,2048]{1,0:T(8,128)(2,1)}, u32[]{:S(2)}, u32[]{:S(2)}) %collective-permute-start.37) | collective-permute-done | bytes 524320 | tf_op jit(solution)/shard_map/ppermute | solution.py:95
  (189 shorter events, 74.6 us)
Async XLA Ops:
  0.6 26.3 %collective-permute-start.24 = (bf16[128,2048]{1,0:T(8,128)(2,1)}, bf16[128,2048]{1,0:T(8,128)(2,1)S(1)}, u32[]{:S(2)}, u32[]{:S(2)}) collective-permute-start(bf16[128,2048]{1,0:T(8,128)(2,1)} %param.13), channel_id=1, source_target_pairs={{0,8},{4,12},{8,0},{12,4},{1,9},{5,13},{9,1},{13,5},{2,10},{6,14},... | collective-permute-start | bytes 1572872 | tf_op jit(solution)/shard_map/ppermute | solution.py:95
  1.0 25.9 %collective-permute-start.25 = (bf16[128,2048]{1,0:T(8,128)(2,1)}, bf16[128,2048]{1,0:T(8,128)(2,1)S(1)}, u32[]{:S(2)}, u32[]{:S(2)}) collective-permute-start(bf16[128,2048]{1,0:T(8,128)(2,1)} %param.13), channel_id=1, source_target_pairs={{0,4},{4,0},{8,12},{12,8},{1,5},{5,1},{9,13},{13,9},{2,6},{6,2},{1... | collective-permute-start | bytes 1572872 | tf_op jit(solution)/shard_map/ppermute | solution.py:95
  1.2 25.7 %collective-permute-start.26 = (bf16[128,2048]{1,0:T(8,128)(2,1)}, bf16[128,2048]{1,0:T(8,128)(2,1)S(1)}, u32[]{:S(2)}, u32[]{:S(2)}) collective-permute-start(bf16[128,2048]{1,0:T(8,128)(2,1)} %param.13), channel_id=1, source_target_pairs={{0,16},{16,0},{1,17},{17,1},{2,18},{18,2},{3,19},{19,3},{4,20},{20... | collective-permute-start | bytes 1572872 | tf_op jit(solution)/shard_map/ppermute | solution.py:95
  3.0 24.8 %collective-permute-start.27 = (bf16[128,2048]{1,0:T(8,128)(2,1)}, bf16[128,2048]{1,0:T(8,128)(2,1)S(1)}, u32[]{:S(2)}, u32[]{:S(2)}) collective-permute-start(bf16[128,2048]{1,0:T(8,128)(2,1)} %param.13), channel_id=1, source_target_pairs={{0,2},{2,0},{1,3},{3,1},{4,6},{6,4},{5,7},{7,5},{8,10},{10,8},{9,1... | collective-permute-start | bytes 1572872 | tf_op jit(solution)/shard_map/ppermute | solution.py:95
  6.0 20.9 %collective-permute-start.28 = (f32[1,16,128]{2,1,0:T(8,128)S(1)}, f32[1,16,128]{2,1,0:T(8,128)S(1)}, u32[]{:S(2)}, u32[]{:S(2)}) collective-permute-start(f32[1,16,128]{2,1,0:T(8,128)S(1)} %select_bitcast_fusion), channel_id=1, source_target_pairs={{0,8},{4,12},{8,0},{12,4},{1,9},{5,13},{9,1},{13,5},{2,10},{6,14},... | collective-permute-start | bytes 24584 | tf_op jit(solution)/shard_map/ppermute | solution.py:95
  30.1 14.4 %collective-permute-start.29 = (bf16[128,2048]{1,0:T(8,128)(2,1)}, bf16[128,2048]{1,0:T(8,128)(2,1)S(1)}, u32[]{:S(2)}, u32[]{:S(2)}) collective-permute-start(bf16[128,2048]{1,0:T(8,128)(2,1)} %copy-done.18), channel_id=1, source_target_pairs={{0,4},{4,0},{8,12},{12,8},{1,5},{5,1},{9,13},{13,9},{2,6},{6,2},{1... | collective-permute-start | bytes 1572872 | tf_op jit(solution)/shard_map/ppermute | solution.py:95
  30.6 13.8 %collective-permute-start.30 = (bf16[128,2048]{1,0:T(8,128)(2,1)}, bf16[128,2048]{1,0:T(8,128)(2,1)S(1)}, u32[]{:S(2)}, u32[]{:S(2)}) collective-permute-start(bf16[128,2048]{1,0:T(8,128)(2,1)} %copy-done.18), channel_id=1, source_target_pairs={{0,16},{16,0},{1,17},{17,1},{2,18},{18,2},{3,19},{19,3},{4,20},{20... | collective-permute-start | bytes 1572872 | tf_op jit(solution)/shard_map/ppermute | solution.py:95
  32.1 13.2 %collective-permute-start.31 = (bf16[128,2048]{1,0:T(8,128)(2,1)}, bf16[128,2048]{1,0:T(8,128)(2,1)S(1)}, u32[]{:S(2)}, u32[]{:S(2)}) collective-permute-start(bf16[128,2048]{1,0:T(8,128)(2,1)} %copy-done.18), channel_id=1, source_target_pairs={{0,2},{2,0},{1,3},{3,1},{4,6},{6,4},{5,7},{7,5},{8,10},{10,8},{9,1... | collective-permute-start | bytes 1572872 | tf_op jit(solution)/shard_map/ppermute | solution.py:95
  33.7 10.8 %collective-permute-start.32 = (f32[2,16,128]{2,1,0:T(8,128)S(1)}, f32[2,16,128]{2,1,0:T(8,128)S(1)}, u32[]{:S(2)}, u32[]{:S(2)}) collective-permute-start(f32[2,16,128]{2,1,0:T(8,128)S(1)} %pad_maximum_fusion.4), channel_id=1, source_target_pairs={{0,4},{4,0},{8,12},{12,8},{1,5},{5,1},{9,13},{13,9},{2,6},{6,2},{1... | collective-permute-start | bytes 49160 | tf_op jit(solution)/shard_map/ppermute | solution.py:95
  46.9 92.0 %collective-permute-start.34 = (bf16[256,4096]{1,0:T(8,128)(2,1)}, bf16[256,4096]{1,0:T(8,128)(2,1)}, u32[]{:S(2)}, u32[]{:S(2)}) collective-permute-start(bf16[256,4096]{1,0:T(8,128)(2,1)} %slice.116), channel_id=1, source_target_pairs={{0,8},{4,12},{8,0},{12,4},{1,9},{5,13},{9,1},{13,5},{2,10},{6,14},... | collective-permute-start | bytes 6291464 | tf_op jit(solution)/shard_map/ppermute | solution.py:95
  49.7 14.9 %collective-permute-start.2 = (bf16[128,2048]{1,0:T(8,128)(2,1)S(1)}, bf16[128,2048]{1,0:T(8,128)(2,1)S(1)}, u32[]{:S(2)}, u32[]{:S(2)}) collective-permute-start(bf16[128,2048]{1,0:T(8,128)(2,1)S(1)} %get-tuple-element.46), channel_id=1, source_target_pairs={{0,16},{16,0},{1,17},{17,1},{2,18},{18,2},{3,19},{19,3},{4,20},{20... | collective-permute-start | bytes 1572872 | tf_op jit(solution)/shard_map/cond/branch_1_fun/ppermute | solution.py:95
  50.2 14.4 %collective-permute-start.3 = (bf16[128,2048]{1,0:T(8,128)(2,1)S(1)}, bf16[128,2048]{1,0:T(8,128)(2,1)S(1)}, u32[]{:S(2)}, u32[]{:S(2)}) collective-permute-start(bf16[128,2048]{1,0:T(8,128)(2,1)S(1)} %get-tuple-element.46), channel_id=1, source_target_pairs={{0,2},{2,0},{1,3},{3,1},{4,6},{6,4},{5,7},{7,5},{8,10},{10,8},{9,1... | collective-permute-start | bytes 1572872 | tf_op jit(solution)/shard_map/cond/branch_1_fun/ppermute | solution.py:95
  51.8 21.0 %collective-permute-start.4 = (bf16[128,2048]{1,0:T(8,128)(2,1)S(1)}, bf16[128,2048]{1,0:T(8,128)(2,1)S(1)}, u32[]{:S(2)}, u32[]{:S(2)}) collective-permute-start(bf16[128,2048]{1,0:T(8,128)(2,1)S(1)} %get-tuple-element.47), channel_id=1, source_target_pairs={{0,16},{16,0},{1,17},{17,1},{2,18},{18,2},{3,19},{19,3},{4,20},{20... | collective-permute-start | bytes 1572872 | tf_op jit(solution)/shard_map/cond/branch_1_fun/ppermute | solution.py:95
  72.8 11.4 %collective-permute-start.7 = (bf16[128,2048]{1,0:T(8,128)(2,1)S(1)}, bf16[128,2048]{1,0:T(8,128)(2,1)S(1)}, u32[]{:S(2)}, u32[]{:S(2)}) collective-permute-start(bf16[128,2048]{1,0:T(8,128)(2,1)S(1)} %get-tuple-element.50), channel_id=1, source_target_pairs={{0,16},{16,0},{1,17},{17,1},{2,18},{18,2},{3,19},{19,3},{4,20},{20... | collective-permute-start | bytes 1572872 | tf_op jit(solution)/shard_map/cond/branch_1_fun/ppermute | solution.py:95
  74.1 14.9 %collective-permute-start.8 = (bf16[128,2048]{1,0:T(8,128)(2,1)S(1)}, bf16[128,2048]{1,0:T(8,128)(2,1)S(1)}, u32[]{:S(2)}, u32[]{:S(2)}) collective-permute-start(bf16[128,2048]{1,0:T(8,128)(2,1)S(1)} %get-tuple-element.50), channel_id=1, source_target_pairs={{0,2},{2,0},{1,3},{3,1},{4,6},{6,4},{5,7},{7,5},{8,10},{10,8},{9,1... | collective-permute-start | bytes 1572872 | tf_op jit(solution)/shard_map/cond/branch_1_fun/ppermute | solution.py:95
  75.6 21.2 %collective-permute-start.6 = (bf16[128,2048]{1,0:T(8,128)(2,1)S(1)}, bf16[128,2048]{1,0:T(8,128)(2,1)S(1)}, u32[]{:S(2)}, u32[]{:S(2)}) collective-permute-start(bf16[128,2048]{1,0:T(8,128)(2,1)S(1)} %collective-permute-done.2), channel_id=1, source_target_pairs={{0,2},{2,0},{1,3},{3,1},{4,6},{6,4},{5,7},{7,5},{8,10},{10,8},{9,1... | collective-permute-start | bytes 1572872 | tf_op jit(solution)/shard_map/cond/branch_1_fun/ppermute | solution.py:95
  99.8 17.0 %collective-permute-start.13 = (bf16[384,2048]{1,0:T(8,128)(2,1)}, bf16[384,2048]{1,0:T(8,128)(2,1)}, u32[]{:S(2)}, u32[]{:S(2)}) collective-permute-start(bf16[384,2048]{1,0:T(8,128)(2,1)} %get-tuple-element.66), channel_id=1, source_target_pairs={{0,1},{1,0},{2,3},{3,2},{4,5},{5,4},{6,7},{7,6},{8,9},{9,8},{10,11... | collective-permute-start | bytes 4718600 | tf_op jit(solution)/shard_map/cond/branch_1_fun/ppermute | solution.py:95
  100.4 16.4 %collective-permute-start.10 = (bf16[128,2048]{1,0:T(8,128)(2,1)}, bf16[128,2048]{1,0:T(8,128)(2,1)}, u32[]{:S(2)}, u32[]{:S(2)}) collective-permute-start(bf16[128,2048]{1,0:T(8,128)(2,1)} %get-tuple-element.57), channel_id=1, source_target_pairs={{0,2},{2,0},{1,3},{3,1},{4,6},{6,4},{5,7},{7,5},{8,10},{10,8},{9,1... | collective-permute-start | bytes 1572872 | tf_op jit(solution)/shard_map/cond/branch_1_fun/ppermute | solution.py:95
  101.9 14.9 %collective-permute-start.11 = (bf16[128,2048]{1,0:T(8,128)(2,1)}, bf16[128,2048]{1,0:T(8,128)(2,1)}, u32[]{:S(2)}, u32[]{:S(2)}) collective-permute-start(bf16[128,2048]{1,0:T(8,128)(2,1)} %copy-done.29), channel_id=1, source_target_pairs={{0,16},{16,0},{1,17},{17,1},{2,18},{18,2},{3,19},{19,3},{4,20},{20... | collective-permute-start | bytes 1572872 | tf_op jit(solution)/shard_map/cond/branch_1_fun/ppermute | solution.py:95
  138.9 129.7 %collective-permute-start.36 = (bf16[384,2048]{1,0:T(8,128)(2,1)}, bf16[384,2048]{1,0:T(8,128)(2,1)}, u32[]{:S(2)}, u32[]{:S(2)}) collective-permute-start(bf16[384,2048]{1,0:T(8,128)(2,1)} %bitcast_select_fusion.2), channel_id=1, source_target_pairs={{0,8},{4,12},{8,0},{12,4},{1,9},{5,13},{9,1},{13,5},{2,10},{6,14},... | collective-permute-start | bytes 4718600 | tf_op jit(solution)/shard_map/ppermute | solution.py:95
  138.9 129.7 %collective-permute-start.35 = (bf16[128,4096]{1,0:T(8,128)(2,1)}, bf16[128,4096]{1,0:T(8,128)(2,1)}, u32[]{:S(2)}, u32[]{:S(2)}) collective-permute-start(bf16[128,4096]{1,0:T(8,128)(2,1)} %slice.117), channel_id=1, source_target_pairs={{0,8},{4,12},{8,0},{12,4},{1,9},{5,13},{9,1},{13,5},{2,10},{6,14},... | collective-permute-start | bytes 3145736 | tf_op jit(solution)/shard_map/ppermute | solution.py:95
  142.7 17.5 %collective-permute-start.20 = (bf16[2,4,128,2048]{3,2,1,0:T(8,128)(2,1)}, bf16[2,4,128,2048]{3,2,1,0:T(8,128)(2,1)}, u32[]{:S(2)}, u32[]{:S(2)}) collective-permute-start(bf16[2,4,128,2048]{3,2,1,0:T(8,128)(2,1)} %get-tuple-element.78.x_ref), channel_id=1, source_target_pairs={{0,1},{1,0},{2,3},{3,2},{4,5},{5,4},{6,7},{7,6},{8,9},{9,8},{10,11... | collective-permute-start | bytes 12582920 | tf_op jit(solution)/shard_map/cond/branch_1_fun/ppermute | solution.py:95
  160.2 19.9 %collective-permute-start.16 = (bf16[512,2048]{1,0:T(8,128)(2,1)}, bf16[512,2048]{1,0:T(8,128)(2,1)}, u32[]{:S(2)}, u32[]{:S(2)}) collective-permute-start(bf16[512,2048]{1,0:T(8,128)(2,1)} %down.5), channel_id=1, source_target_pairs={{0,1},{1,0},{2,3},{3,2},{4,5},{5,4},{6,7},{7,6},{8,9},{9,8},{10,11... | collective-permute-start | bytes 6291464 | tf_op jit(solution)/shard_map/cond/branch_1_fun/ppermute | solution.py:95
  165.9 11.5 %collective-permute-start.21 = (bf16[512,384]{1,0:T(8,128)(2,1)S(1)}, bf16[512,384]{1,0:T(8,128)(2,1)S(1)}, u32[]{:S(2)}, u32[]{:S(2)}) collective-permute-start(bf16[512,384]{1,0:T(8,128)(2,1)S(1)} %project.7.own_ref), channel_id=1, source_target_pairs={{0,16},{16,0},{1,17},{17,1},{2,18},{18,2},{3,19},{19,3},{4,20},{20... | collective-permute-start | bytes 1179656 | tf_op jit(solution)/shard_map/cond/branch_1_fun/ppermute | solution.py:95
  180.0 31.5 %collective-permute-start.22 = (bf16[512,2048]{1,0:T(8,128)(2,1)S(1)}, bf16[512,2048]{1,0:T(8,128)(2,1)}, u32[]{:S(2)}, u32[]{:S(2)}) collective-permute-start(bf16[512,2048]{1,0:T(8,128)(2,1)S(1)} %down.7), channel_id=1, source_target_pairs={{0,1},{1,0},{2,3},{3,2},{4,5},{5,4},{6,7},{7,6},{8,9},{9,8},{10,11... | collective-permute-start | bytes 6291464 | tf_op jit(solution)/shard_map/cond/branch_1_fun/ppermute | solution.py:95
  184.1 25.9 %collective-permute-start.17 = (bf16[2,128,2048]{2,1,0:T(8,128)(2,1)}, bf16[2,128,2048]{2,1,0:T(8,128)(2,1)}, u32[]{:S(2)}, u32[]{:S(2)}) collective-permute-start(bf16[2,128,2048]{2,1,0:T(8,128)(2,1)} %bitcast.31), channel_id=1, source_target_pairs={{0,2},{2,0},{1,3},{3,1},{4,6},{6,4},{5,7},{7,5},{8,10},{10,8},{9,1... | collective-permute-start | bytes 3145736 | tf_op jit(solution)/shard_map/cond/branch_1_fun/ppermute | solution.py:95
  185.6 11.2 %collective-permute-start.19 = (bf16[512,384]{1,0:T(8,128)(2,1)S(1)}, bf16[512,384]{1,0:T(8,128)(2,1)S(1)}, u32[]{:S(2)}, u32[]{:S(2)}) collective-permute-start(bf16[512,384]{1,0:T(8,128)(2,1)S(1)} %project.6.own_ref), channel_id=1, source_target_pairs={{0,16},{16,0},{1,17},{17,1},{2,18},{18,2},{3,19},{19,3},{4,20},{20... | collective-permute-start | bytes 1179656 | tf_op jit(solution)/shard_map/cond/branch_1_fun/ppermute | solution.py:95
  213.9 51.7 %collective-permute-start.23 = (bf16[2,128,2048]{2,1,0:T(8,128)(2,1)S(1)}, bf16[2,128,2048]{2,1,0:T(8,128)(2,1)S(1)}, u32[]{:S(2)}, u32[]{:S(2)}) collective-permute-start(bf16[2,128,2048]{2,1,0:T(8,128)(2,1)S(1)} %bitcast.95), channel_id=1, source_target_pairs={{0,2},{2,0},{1,3},{3,1},{4,6},{6,4},{5,7},{7,5},{8,10},{10,8},{9,1... | collective-permute-start | bytes 3145736 | tf_op jit(solution)/shard_map/cond/branch_1_fun/ppermute | solution.py:95
  215.5 49.2 %collective-permute-start.18 = (bf16[128,2048]{1,0:T(8,128)(2,1)S(1)}, bf16[128,2048]{1,0:T(8,128)(2,1)S(1)}, u32[]{:S(2)}, u32[]{:S(2)}) collective-permute-start(bf16[128,2048]{1,0:T(8,128)(2,1)S(1)} %slice_bitcast_fusion.1), channel_id=1, source_target_pairs={{0,4},{4,0},{8,12},{12,8},{1,5},{5,1},{9,13},{13,9},{2,6},{6,2},{1... | collective-permute-start | bytes 1572872 | tf_op jit(solution)/shard_map/cond/branch_1_fun/ppermute | solution.py:95
  267.8 10.7 %collective-permute-start.39 = (bf16[256,4096]{1,0:T(8,128)(2,1)}, bf16[256,4096]{1,0:T(8,128)(2,1)S(1)}, u32[]{:S(2)}, u32[]{:S(2)}) collective-permute-start(bf16[256,4096]{1,0:T(8,128)(2,1)} %collective-permute-done.34), channel_id=1, source_target_pairs={{0,1},{1,0},{2,3},{3,2},{4,5},{5,4},{6,7},{7,6},{8,9},{9,8},{10,11... | collective-permute-start | bytes 6291464 | tf_op jit(solution)/shard_map/ppermute | solution.py:95
  269.1 25.8 %collective-permute-start.37 = (bf16[128,2048]{1,0:T(8,128)(2,1)}, bf16[128,2048]{1,0:T(8,128)(2,1)}, u32[]{:S(2)}, u32[]{:S(2)}) collective-permute-start(bf16[128,2048]{1,0:T(8,128)(2,1)} %get-tuple-element.161), channel_id=1, source_target_pairs={{0,8},{4,12},{8,0},{12,4},{1,9},{5,13},{9,1},{13,5},{2,10},{6,14},... | collective-permute-start | bytes 1572872 | tf_op jit(solution)/shard_map/ppermute | solution.py:95
  269.1 25.8 %collective-permute-start.38 = (bf16[128,2048]{1,0:T(8,128)(2,1)}, bf16[128,2048]{1,0:T(8,128)(2,1)}, u32[]{:S(2)}, u32[]{:S(2)}) collective-permute-start(bf16[128,2048]{1,0:T(8,128)(2,1)} %get-tuple-element.162), channel_id=1, source_target_pairs={{0,4},{4,0},{8,12},{12,8},{1,5},{5,1},{9,13},{13,9},{2,6},{6,2},{1... | collective-permute-start | bytes 1572872 | tf_op jit(solution)/shard_map/ppermute | solution.py:95
  (47 other events, 529.2 us)

commit v2 on v1

--- a/solution.py
+++ b/solution.py
@@ -118,38 +118,38 @@
     return wide(kept[0]) + wide(received[0]), hop(leave, "y")
 
 
-def gather_stage(tokens, near, far, apart, across_0, beside_0, across_2, beside_2, table, tail, w_pair):
-    rows = tokens.shape[0]
+def gather_stage(tokens, near, far, apart, tail, w_pair):
     part = lax.axis_index("dp").astype(jnp.int32).reshape(1)
-    mine = jnp.arange(table.shape[1], dtype=jnp.int32) == lax.axis_index(COLUMN)
-    across_3, beside_3, corner_2, table_y, near = tie(
-        hop(apart, "dp"), hop(apart, "y"), hop(beside_2, "dp"), hop(table, "y"), near
-    )
-    table = jnp.concatenate([table, table_y])
-    corner_3, across_1, beside_1, table_core, across_0, tail = tie(
-        hop(across_3, "y"), hop(near, "dp"), hop(near, "y"), hop(table, "core"), across_0, tail
-    )
-    table = jnp.concatenate([table, table_core])
+    across_2, beside_2, across_3, beside_3, near = tie(
+        hop(far, "dp"), hop(far, "y"), hop(apart, "dp"), hop(apart, "y"), near
+    )
+    corner_2, corner_3, across_1, beside_1, tokens, tail = tie(
+        hop(beside_2, "dp"), hop(across_3, "y"), hop(near, "dp"), hop(near, "y"), tokens, tail
+    )
+    across_0, beside_0, tail = hop(tokens, "dp"), hop(tokens, "y"), hop(tail, "core")
     own = jnp.stack([far, apart, beside_2, beside_3])
     x_late = jnp.stack([own, jnp.stack([across_2, across_3, corner_2, corner_3])])
     x_late_other = hop(x_late, "core")
+    late_own = project(part, x_late, w_pair, 4)
+    across_0, beside_0, tail, late_own, beside_1 = tie(across_0, beside_0, tail, late_own, beside_1)
+    corner_0, corner_1 = hop(across_0, "y"), hop(beside_1, "dp")
+    late_other = project(part, x_late_other, w_pair, 4)
+    corner_0, corner_1, late_own, late_other = tie(corner_0, corner_1, late_own, late_other)
+    own = jnp.stack([tokens, near, beside_0, beside_1])
+    x_early = jnp.stack([own, jnp.stack([across_0, across_1, corner_0, corner_1])])
+    return x_early, late_own, hop(late_own, "dp"), late_other, tail
+
+
+def expert_stage(x_early, late_own, late_own_cross, late_other, table, w_pair, w_down):
+    rows = x_early.shape[2]
+    part = lax.axis_index("dp").astype(jnp.int32).reshape(1)
+    mine = jnp.arange(table.shape[1], dtype=jnp.int32) == lax.axis_index(COLUMN)
+    for axis in ("y", "core"):
+        table = jnp.concatenate([table, hop(table, axis)])
     counts = jnp.sum((table >= 0).astype(jnp.float32), axis=(0, 2))
     scale = jnp.sum(jnp.where(mine[None, :, None], jnp.maximum(table, 0.0), 0.0), axis=1)
     scale = scale.reshape(2, 2, 2, 2, rows).transpose(0, 3, 1, 2, 4)
     scale = scale.reshape(2, 2, 4 * rows, 1)
-    corner_0, corner_1 = hop(across_0, "y"), hop(beside_1, "dp")
-    late_own = project(part, x_late, w_pair, 4)
-    late_other = project(part, x_late_other, w_pair, 4)
-    corner_0, corner_1, late_own, late_other, scale, tail = tie(
-        corner_0, corner_1, late_own, late_other, scale, hop(tail, "core")
-    )
-    own = jnp.stack([tokens, near, beside_0, beside_1])
-    x_early = jnp.stack([own, jnp.stack([across_0, across_1, corner_0, corner_1])])
-    return x_early, late_own, hop(late_own, "dp"), late_other, scale, counts, tail
-
-
-def expert_stage(x_early, late_own, late_own_cross, late_other, scale, w_pair, w_down):
-    part = lax.axis_index("dp").astype(jnp.int32).reshape(1)
     late_other_cross = hop(late_other, "dp")
     x_early_other = hop(x_early, "core")
     early_own = project(part, x_early, w_pair, 4)
@@ -164,7 +164,7 @@
     line = (wide(line[0]) + wide(hop(line[1], "z", 1))).astype(jnp.bfloat16)
     total, total_y = across_y(*early)
     total = total + wide(total_y)
-    return line, total[0], total[1].astype(jnp.bfloat16)
+    return line, total[0], total[1].astype(jnp.bfloat16), counts
 
 
 def guarded(valid, stage, *operands):
@@ -200,43 +200,36 @@
     table = jnp.where(named, weight, -1.0).T[None]
 
     heads, tails = (w_pair[:hid], w_down[:depth]), (w_pair[hid:], w_down[depth:])
-    far, near, across_0, beside_0, table_far, late_tail = tie(
-        hop(tokens, "z", 2),
-        hop(tokens, "z", 1),
-        hop(tokens, "dp"),
-        hop(tokens, "y"),
-        hop(table, "z", 2),
-        tails[0],
-    )
+    far, near, table_far, crossed = tie(
+        hop(tokens, "z", 2), hop(tokens, "z", 1), hop(table, "z", 2), hop(w_pair, "core")
+    )
+    crossed = crossed[hid:]
     table = jnp.concatenate([table, table_far])
-    lane_pair = jnp.where(own, heads[0], hop(late_tail, "core"))
-    apart, across_2, beside_2, table_near, lane_pair = tie(
-        hop(far, "z", 1),
-        hop(far, "dp"),
-        hop(far, "y"),
-        hop(table, "z", 1),
-        lane_pair,
+    mark = 19 * hid // 24
+    lane_first = jnp.where(own, heads[0][:mark], crossed[:mark])
+    lane_second = jnp.where(own, heads[0][mark:], crossed[mark:])
+    apart, table_near, lane_first, lane_second = tie(
+        hop(far, "z", 1), hop(table, "z", 1), lane_first, lane_second
     )
     table = jnp.concatenate([table, table_near])
-    mark = 2 * hid // 3
-    arrived_first = hop(lane_pair[:mark], "z", 2)
+    arrived_first = hop(lane_first, "z", 2)
 
     valid = placement[0] >= 0
-    planes = (tokens, near, far, apart, across_0, beside_0, across_2, beside_2)
-    *staged, counts, tail_down = guarded(valid, gather_stage, *planes, table, tails[1], w_pair)
+    *staged, tail_down = guarded(
+        valid, gather_stage, tokens, near, far, apart, tails[1], w_pair
+    )
     lane_down = jnp.where(own, heads[1], tail_down)
     *staged, arrived_first, lane_second, lane_down = tie(
-        *staged, arrived_first, lane_pair[mark:], lane_down
+        *staged, arrived_first, lane_second, lane_down
     )
     arrived_second, arrived_down = hop(lane_second, "z", 2), hop(lane_down, "z", 2)
-    handed_first = hop(arrived_first, "core")
-    line, total, leave = guarded(valid, expert_stage, *staged, w_pair, w_down)
-    line, total, leave, arrived_second, arrived_down = tie(
-        line, total, leave, arrived_second, arrived_down
+    line, total, leave, counts = guarded(valid, expert_stage, *staged, table, w_pair, w_down)
+    line, total, leave, arrived_first, arrived_second, arrived_down = tie(
+        line, total, leave, arrived_first, arrived_second, arrived_down
     )
     over, closing = hop(line, "z", 2), hop(leave, "z", 1)
     handed_first, handed_second, handed_down, *last = tie(
-        handed_first, hop(arrived_second, "core"), hop(arrived_down, "core"), *tails
+        *(hop(value, "core") for value in (arrived_first, arrived_second, arrived_down)), w_pair, w_down
     )
     partner = (slots + half * jnp.tile(swap_flag, 2)) % ncol
     column_load = jnp.sum(
@@ -244,7 +237,10 @@
     ) / jnp.float32(rows * topk)
 
     rest = lax.cond(
-        both, lambda a, b: (hop(a, "z", 2), hop(b, "z", 2)), lambda a, b: (a, b), *last
+        both,
+        lambda a, b: (hop(a[hid:], "z", 2), hop(b[depth:], "z", 2)),
+        lambda a, b: (a[hid:], b[depth:]),
+        *last,
     )
     arrived = (jnp.concatenate([arrived_first, arrived_second]), arrived_down)
     handed = (jnp.concatenate([handed_first, handed_second]), handed_down)

time: 302 us -> 297 us (0.983)
  other arithmetic: 43.6 us -> 50.2 us
  local copies, waits for them, and re-layouts: 16.3 us -> 10.4 us
    unnamed x40 -> x18, local copies, waits for them, and re-layouts: 6.11 us -> 0.22 us
    select_n x1 -> x2, other arithmetic: 3.17 us -> 6.35 us  [the longest x1 4.16 us: body(): lane_first = jnp.where(own, heads[0][:mark], crossed[:mark])]
  transfers between devices with their start and end apart: 40 -> 40, of which waited for: 18 -> 21; matrix products, arithmetic and copies ran while one was open for 16% -> 19% of each run, Pallas kernels for 15% -> 15%
where the time goes in v2:
time: 297 us; the launch traced here: 294 us
  waiting for transfers between devices  153 us (52%)
  other arithmetic  50.2 us (17%)
  Pallas kernels  43.7 us (15%)
  starting transfers between devices  33.6 us (11%)
  local copies, waits for them, and re-layouts  10.4 us (4%)
    ppermute x40, waiting for transfers between devices, hop(): lax.ppermute(value, axis, [(p, p ^ mask) for p in range(lax.axis_size(axi...  153 us
    ppermute x40, starting transfers between devices, hop(): lax.ppermute(value, axis, [(p, p ^ mask) for p in range(lax.axis_size(axi...  33.6 us
    pallas_call x4, Pallas kernels, project(): pl.pallas_call(project_kernel, grid_spec=pltpu.PrefetchScalarGridSpec(num...  26.5 us
    pallas_call x4, Pallas kernels, down(): pl.pallas_call(down_kernel, grid_spec=pltpu.PrefetchScalarGridSpec(num_sc...  17.2 us
    convert_element_type x2, other arithmetic, across_y(): leave = (wide(kept[1]) + wide(received[1])).astype(jnp.bfloat16)  6.32 us
    select_n x2, other arithmetic, body(): heads = [jnp.where(own, new, old) for new, old in zip(arrived, heads)]  6.1 us
  transfers between devices with their start and end apart: 40, of which 21 were waited for; matrix products, arithmetic and copies ran while one was open for 19% of the time, Pallas kernels for 15%

profile of v2, /device:TPU:24, one launch (start us, length us, event | category | flops | bytes accessed | tf_op | source)
XLA Modules:
  0.0 293.6 jit_solution(11073232542038249881)
XLA Ops:
  2.8 2.9 collective-permute-start.30
  8.3 19.4 %collective-permute-done.30 = f32[1,16,128]{2,1,0:T(8,128)S(1)} collective-permute-done((f32[1,16,128]{2,1,0:T(8,128)S(1)}, f32[1,16,128]{2,1,0:T(8,128)S(1)}, u32[]{:S(2)}, u32[]{:S(2)}) %collective-permute-start.30) | collective-permute-done | bytes 8224 | tf_op jit(solution)/shard_map/ppermute | solution.py:95
  29.8 4.2 %bitcast_select_fusion = bf16[304,4096]{1,0:T(8,128)(2,1)} fusion(bf16[768,4096]{1,0:T(8,128)(2,1)} %collective-permute-done.31, bf16[1,2,384,4096]{3,2,1,0:T(8,128)(2,1)} %param.18, pred[]{:T(512)S(6)} %eq.80), kind=kLoop, calls=%fused_computation.36 | loop fusion | flops 1245184 | bytes 7471105 | tf_op jit(solution)/shard_map/jit(_where)/select_n | solution.py:209
  36.1 5.8 %collective-permute-done.32 = bf16[128,2048]{1,0:T(8,128)(2,1)S(1)} collective-permute-done((bf16[128,2048]{1,0:T(8,128)(2,1)S(1)}, bf16[128,2048]{1,0:T(8,128)(2,1)S(1)}, u32[]{:S(2)}, u32[]{:S(2)}) %collective-permute-start.32) | collective-permute-done | bytes 524320 | tf_op jit(solution)/shard_map/ppermute | solution.py:95
  42.1 90.4 %conditional.3 = (bf16[2,4,128,2048]{3,2,1,0:T(8,128)(2,1)}, bf16[512,384]{1,0:T(8,128)(2,1)}, bf16[512,384]{1,0:T(8,128)(2,1)}, bf16[512,384]{1,0:T(8,128)(2,1)S(1)}, bf16[384,2048]{1,0:T(8,128)(2,1)}) conditional(s32[]{:T(128)} %bitcast.41, () %tuple.46, (bf16[128,2048]{1,0:T(8,128)(2,1)S(1)}, bf16[128,2048]{1,0:T(8,128)(2,1)S(1)}, ...), branch_computations={%region_4.5_spmd, %region_5.6_spmd} | conditional | flops 6459228160 | bytes 140510080 | solution.py:173
  46.3 10.8 %collective-permute-done.3 = bf16[128,2048]{1,0:T(8,128)(2,1)S(1)} collective-permute-done((bf16[128,2048]{1,0:T(8,128)(2,1)S(1)}, bf16[128,2048]{1,0:T(8,128)(2,1)S(1)}, u32[]{:S(2)}, u32[]{:S(2)}) %collective-permute-start.3) | collective-permute-done | bytes 524320 | tf_op jit(solution)/shard_map/cond/branch_1_fun/ppermute | solution.py:95
  58.5 7.6 %collective-permute-done.5 = bf16[128,2048]{1,0:T(8,128)(2,1)S(1)} collective-permute-done((bf16[128,2048]{1,0:T(8,128)(2,1)S(1)}, bf16[128,2048]{1,0:T(8,128)(2,1)S(1)}, u32[]{:S(2)}, u32[]{:S(2)}) %collective-permute-start.5) | collective-permute-done | bytes 524320 | tf_op jit(solution)/shard_map/cond/branch_1_fun/ppermute | solution.py:95
  73.0 17.4 %collective-permute-done.6 = bf16[128,2048]{1,0:T(8,128)(2,1)S(1)} collective-permute-done((bf16[128,2048]{1,0:T(8,128)(2,1)S(1)}, bf16[128,2048]{1,0:T(8,128)(2,1)S(1)}, u32[]{:S(2)}, u32[]{:S(2)}) %collective-permute-start.6) | collective-permute-done | bytes 524320 | tf_op jit(solution)/shard_map/cond/branch_1_fun/ppermute | solution.py:95
  97.4 7.6 %project.4 = bf16[512,384]{1,0:T(8,128)(2,1)S(1)} custom-call(s32[1]{0:T(128)} %bitcast.3.part_ref, bf16[2,4,128,2048]{3,2,1,0:T(8,128)(2,1)} %pad_maximum_fusion.x_ref, bf16[768,4096]{1,0:T(8,128)(2,1)} %get-tuple-element.50.own_w_ref.other_w_ref, bf16[768,4096]{1,0:T(8,128)(2,1)} %get-tuple-element.50.own_w_ref.other_w_ref), custom_call_target="tpu_custom_call" | custom-call | flops 3221225472 | bytes 10485760 | tf_op jit(solution)/shard_map/cond/branch_1_fun/project/pallas_call | solution.py:36
  105.1 3.3 %collective-permute-done.11 = bf16[128,2048]{1,0:T(8,128)(2,1)} collective-permute-done((bf16[128,2048]{1,0:T(8,128)(2,1)S(1)}, bf16[128,2048]{1,0:T(8,128)(2,1)}, u32[]{:S(2)}, u32[]{:S(2)}) %collective-permute-start.11) | collective-permute-done | bytes 524320 | tf_op jit(solution)/shard_map/cond/branch_1_fun/ppermute | solution.py:95
  113.0 5.7 %project.5 = bf16[512,384]{1,0:T(8,128)(2,1)S(1)} custom-call(s32[1]{0:T(128)} %bitcast.3.part_ref, bf16[2,4,128,2048]{3,2,1,0:T(8,128)(2,1)} %collective-permute-done.15.x_ref, bf16[768,4096]{1,0:T(8,128)(2,1)S(1)} %bitcast.87, bf16[768,4096]{1,0:T(8,128)(2,1)S(1)} %bitcast.87), custom_call_target="tpu_custom_call" | custom-call | flops 3221225472 | bytes 10485760 | tf_op jit(solution)/shard_map/cond/branch_1_fun/project/pallas_call | solution.py:36
  118.7 3.5 %collective-permute-done.14 = bf16[128,2048]{1,0:T(8,128)(2,1)S(1)} collective-permute-done((bf16[128,2048]{1,0:T(8,128)(2,1)S(1)}, bf16[128,2048]{1,0:T(8,128)(2,1)S(1)}, u32[]{:S(2)}, u32[]{:S(2)}) %collective-permute-start.14) | collective-permute-done | bytes 524320 | tf_op jit(solution)/shard_map/cond/branch_1_fun/ppermute | solution.py:95
  127.9 4.6 %collective-permute-done.16 = bf16[512,384]{1,0:T(8,128)(2,1)} collective-permute-done((bf16[512,384]{1,0:T(8,128)(2,1)S(1)}, bf16[512,384]{1,0:T(8,128)(2,1)}, u32[]{:S(2)}, u32[]{:S(2)}) %collective-permute-start.16) | collective-permute-done | bytes 393248 | tf_op jit(solution)/shard_map/cond/branch_1_fun/ppermute | solution.py:95
  132.5 3.2 %bitcast_select_fusion.2 = bf16[384,2048]{1,0:T(8,128)(2,1)} fusion(bf16[384,2048]{1,0:T(8,128)(2,1)} %get-tuple-element.132, pred[]{:T(512)S(6)} %eq.80, bf16[1,768,2048]{2,1,0:T(8,128)(2,1)} %param.19), kind=kLoop, calls=%fused_computation.38 | loop fusion | flops 786432 | bytes 4718593 | tf_op jit(solution)/shard_map/jit(_where)/select_n | solution.py:221
  135.8 15.6 %collective-permute-done.34 = bf16[304,4096]{1,0:T(8,128)(2,1)} collective-permute-done((bf16[304,4096]{1,0:T(8,128)(2,1)}, bf16[304,4096]{1,0:T(8,128)(2,1)}, u32[]{:S(2)}, u32[]{:S(2)}) %collective-permute-start.34) | collective-permute-done | bytes 2490400 | tf_op jit(solution)/shard_map/ppermute | solution.py:95
  151.4 2.9 collective-permute-start.35
  154.3 108.9 %conditional.4 = (bf16[128,2048]{1,0:T(8,128)(2,1)}, f32[128,2048]{1,0:T(8,128)}, bf16[128,2048]{1,0:T(8,128)(2,1)}, f32[16]{0:T(128)S(1)}) conditional(s32[]{:T(128)} %bitcast.41, () %tuple.43, (f32[4,16,128]{2,1,0:T(8,128)S(1)}, bf16[512,384]{1,0:T(8,128)(2,1)}, bf16[512,384]{1,0:T(8,128)(2,1)}, bf16[768,2048]{1,0:T(8,128)(2,1)}, ...), branch_computations={%region_6.7_spmd, %region_7.10_spmd} | conditional | flops 12896122880 | bytes 172401472 | solution.py:173
  157.7 7.5 %project.6.own_ref = bf16[512,384]{1,0:T(8,128)(2,1)S(1)} custom-call(s32[1]{0:T(128)} %bitcast.22.part_ref, bf16[2,4,128,2048]{3,2,1,0:T(8,128)(2,1)} %get-tuple-element.67.x_ref, bf16[768,4096]{1,0:T(8,128)(2,1)} %get-tuple-element.68.own_w_ref.other_w_ref, bf16[768,4096]{1,0:T(8,128)(2,1)} %get-tuple-element.68.own_w_ref.other_w_ref), custom_call_target="tpu_custom_call" | custom-call | flops 3221225472 | bytes 10485760 | tf_op jit(solution)/shard_map/cond/branch_1_fun/project/pallas_call | solution.py:36
  167.3 5.5 %down.5 = bf16[512,2048]{1,0:T(8,128)(2,1)} custom-call(s32[1]{0:T(128)} %bitcast.22.part_ref, bf16[512,384]{1,0:T(8,128)(2,1)S(1)} %get-tuple-element.69.own_ref, bf16[512,384]{1,0:T(8,128)(2,1)S(1)} %collective-permute-done.19.other_ref, bf16[768,2048]{1,0:T(8,128)(2,1)} %get-tuple-element.64.own_w_ref.other_w_ref, ...), custom_call_target="tpu_custom_call" | custom-call | flops 1610612736 | bytes 6029312 | tf_op jit(solution)/shard_map/cond/branch_1_fun/down/pallas_call | solution.py:69
  172.9 5.7 %project.7.own_ref = bf16[512,384]{1,0:T(8,128)(2,1)S(1)} custom-call(s32[1]{0:T(128)} %bitcast.22.part_ref, bf16[2,4,128,2048]{3,2,1,0:T(8,128)(2,1)} %collective-permute-done.24.x_ref, bf16[768,4096]{1,0:T(8,128)(2,1)S(1)} %copy-done, bf16[768,4096]{1,0:T(8,128)(2,1)S(1)} %copy-done), custom_call_target="tpu_custom_call" | custom-call | flops 3221225472 | bytes 10485760 | tf_op jit(solution)/shard_map/cond/branch_1_fun/project/pallas_call | solution.py:36
  180.5 4.7 %down.4 = bf16[512,2048]{1,0:T(8,128)(2,1)S(1)} custom-call(s32[1]{0:T(128)} %bitcast.22.part_ref, bf16[512,384]{1,0:T(8,128)(2,1)S(1)} %copy-done.8, bf16[512,384]{1,0:T(8,128)(2,1)} %get-tuple-element.63.other_ref, bf16[768,2048]{1,0:T(8,128)(2,1)} %get-tuple-element.64.own_w_ref.other_w_ref, bf16[768,2048]{1,0:T(8,128)(2,1)} %get-tuple-element.64.own_w_ref.other_w_ref, ...), custom_call_target="tpu_custom_call" | custom-call | flops 1610612736 | bytes 6029312 | tf_op jit(solution)/shard_map/cond/branch_1_fun/down/pallas_call | solution.py:69
  185.2 4.9 %collective-permute-done.25.other_ref = bf16[512,384]{1,0:T(8,128)(2,1)S(1)} collective-permute-done((bf16[512,384]{1,0:T(8,128)(2,1)S(1)}, bf16[512,384]{1,0:T(8,128)(2,1)S(1)}, u32[]{:S(2)}, u32[]{:S(2)}) %collective-permute-start.25) | collective-permute-done | bytes 393248 | tf_op jit(solution)/shard_map/cond/branch_1_fun/ppermute | solution.py:95
  192.8 4.0 %add_convert_fusion.2 = (bf16[256,2048]{1,0:T(8,128)(2,1)}, f32[256,2048]{1,0:T(8,128)}) fusion(bf16[512,2048]{1,0:T(8,128)(2,1)} %collective-permute-done.20, bf16[512,2048]{1,0:T(8,128)(2,1)S(1)} %down.4), kind=kLoop, calls=%fused_computation.11 | loop fusion | flops 3670016 | bytes 7340032 | tf_op jit(solution)/shard_map/cond/branch_1_fun/convert_element_type | solution.py:117
  198.9 9.6 %collective-permute-done.23.other_ref = bf16[512,384]{1,0:T(8,128)(2,1)S(1)} collective-permute-done((bf16[512,384]{1,0:T(8,128)(2,1)S(1)}, bf16[512,384]{1,0:T(8,128)(2,1)S(1)}, u32[]{:S(2)}, u32[]{:S(2)}) %collective-permute-start.23) | collective-permute-done | bytes 393248 | tf_op jit(solution)/shard_map/cond/branch_1_fun/ppermute | solution.py:95
  208.5 4.4 %down.6 = bf16[512,2048]{1,0:T(8,128)(2,1)S(1)} custom-call(s32[1]{0:T(128)} %bitcast.22.part_ref, bf16[512,384]{1,0:T(8,128)(2,1)S(1)} %project.6.own_ref, bf16[512,384]{1,0:T(8,128)(2,1)S(1)} %collective-permute-done.23.other_ref, bf16[768,2048]{1,0:T(8,128)(2,1)} %get-tuple-element.64.own_w_ref.other_w_ref, ...), custom_call_target="tpu_custom_call" | custom-call | flops 1610612736 | bytes 6029312 | tf_op jit(solution)/shard_map/cond/branch_1_fun/down/pallas_call | solution.py:69
  212.9 9.7 %collective-permute-done.21 = bf16[2,128,2048]{2,1,0:T(8,128)(2,1)} collective-permute-done((bf16[2,128,2048]{2,1,0:T(8,128)(2,1)}, bf16[2,128,2048]{2,1,0:T(8,128)(2,1)}, u32[]{:S(2)}, u32[]{:S(2)}) %collective-permute-start.21) | collective-permute-done | bytes 1048608 | tf_op jit(solution)/shard_map/cond/branch_1_fun/ppermute | solution.py:95
  227.2 32.8 %collective-permute-done.22 = bf16[128,2048]{1,0:T(8,128)(2,1)S(1)} collective-permute-done((bf16[128,2048]{1,0:T(8,128)(2,1)S(1)}, bf16[128,2048]{1,0:T(8,128)(2,1)S(1)}, u32[]{:S(2)}, u32[]{:S(2)}) %collective-permute-start.22) | collective-permute-done | bytes 524320 | tf_op jit(solution)/shard_map/cond/branch_1_fun/ppermute | solution.py:95
  267.9 4.8 %maximum_select_fusion = bf16[1,384,4096]{2,1,0:T(8,128)(2,1)} fusion(bf16[1,80,4096]{2,1,0:T(8,128)(2,1)} %bitcast.51, bf16[1,304,4096]{2,1,0:T(8,128)(2,1)} %bitcast.50, bf16[1,2,384,4096]{3,2,1,0:T(8,128)(2,1)} %param.18, pred[]{:T(512)S(6)} %eq.80), kind=kLoop, calls=%fused_computation.32 | loop fusion | flops 7864320 | bytes 9437185 | tf_op jit(solution)/shard_map/jit(_where)/select_n | solution.py:247
  274.1 5.2 %conditional.5 = (bf16[384,4096]{1,0:T(8,128)(2,1)}, bf16[384,2048]{1,0:T(8,128)(2,1)}) conditional(s32[]{:T(128)} %convert_element_type.93, (bf16[768,4096]{1,0:T(8,128)(2,1)}, bf16[768,2048]{1,0:T(8,128)(2,1)S(1)}) %tuple.75, (bf16[768,4096]{1,0:T(8,128)(2,1)}, bf16[768,2048]{1,0:T(8,128)(2,1)S(1)}) %tuple.76), branch_computations={%region_11.12_spmd, %region_12.13_spmd} | conditional | bytes 28311648 | solution.py:239
  275.4 3.9 %slice.113 = bf16[384,4096]{1,0:T(8,128)(2,1)} slice(bf16[768,4096]{1,0:T(8,128)(2,1)} %get-tuple-element.71), slice={[384:768], [0:4096]} | slice | bytes 6291456 | tf_op jit(solution)/shard_map/cond/branch_0_fun/slice | solution.py:242
  283.2 4.0 %fusion.2 = bf16[1,384,4096]{2,1,0:T(8,128)(2,1)S(1)} fusion(bf16[384,4096]{1,0:T(8,128)(2,1)} %get-tuple-element.153, bf16[80,4096]{1,0:T(8,128)(2,1)S(1)} %collective-permute-done.40, bf16[304,4096]{1,0:T(8,128)(2,1)} %collective-permute-done.39, pred[]{:T(512)S(6)} %and.37), kind=kLoop, calls=%fused_computation.34 | loop fusion | flops 7864320 | bytes 9437185 | tf_op jit(solution)/shard_map/stack | solution.py:249
  287.2 3.2 %maximum_bitcast_fusion.4 = bf16[1,2,384,4096]{3,2,1,0:T(8,128)(2,1)} fusion(bf16[1,384,4096]{2,1,0:T(8,128)(2,1)S(1)} %fusion.2, bf16[1,384,4096]{2,1,0:T(8,128)(2,1)S(1)} %copy-done.4), kind=kLoop, calls=%fused_computation.31 | loop fusion | flops 3145728 | bytes 12582912 | tf_op jit(solution)/shard_map/broadcast_in_dim | solution.py:249
  (155 shorter events, 71.5 us)
Async XLA Ops:
  0.6 27.0 %collective-permute-start.31 = (bf16[768,4096]{1,0:T(8,128)(2,1)}, bf16[768,4096]{1,0:T(8,128)(2,1)}, u32[]{:S(2)}, u32[]{:S(2)}) collective-permute-start(bf16[768,4096]{1,0:T(8,128)(2,1)} %bitcast.81), channel_id=1, source_target_pairs={{0,1},{1,0},{2,3},{3,2},{4,5},{5,4},{6,7},{7,6},{8,9},{9,8},{10,11... | collective-permute-start | bytes 18874376 | tf_op jit(solution)/shard_map/ppermute | solution.py:95
  0.7 26.9 %collective-permute-start.28 = (bf16[128,2048]{1,0:T(8,128)(2,1)}, bf16[128,2048]{1,0:T(8,128)(2,1)S(1)}, u32[]{:S(2)}, u32[]{:S(2)}) collective-permute-start(bf16[128,2048]{1,0:T(8,128)(2,1)} %param.13), channel_id=1, source_target_pairs={{0,8},{4,12},{8,0},{12,4},{1,9},{5,13},{9,1},{13,5},{2,10},{6,14},... | collective-permute-start | bytes 1572872 | tf_op jit(solution)/shard_map/ppermute | solution.py:95
  1.1 26.5 %collective-permute-start.29 = (bf16[128,2048]{1,0:T(8,128)(2,1)}, bf16[128,2048]{1,0:T(8,128)(2,1)S(1)}, u32[]{:S(2)}, u32[]{:S(2)}) collective-permute-start(bf16[128,2048]{1,0:T(8,128)(2,1)} %param.13), channel_id=1, source_target_pairs={{0,4},{4,0},{8,12},{12,8},{1,5},{5,1},{9,13},{13,9},{2,6},{6,2},{1... | collective-permute-start | bytes 1572872 | tf_op jit(solution)/shard_map/ppermute | solution.py:95
  2.8 24.8 %collective-permute-start.30 = (f32[1,16,128]{2,1,0:T(8,128)S(1)}, f32[1,16,128]{2,1,0:T(8,128)S(1)}, u32[]{:S(2)}, u32[]{:S(2)}) collective-permute-start(f32[1,16,128]{2,1,0:T(8,128)S(1)} %select_bitcast_fusion), channel_id=1, source_target_pairs={{0,8},{4,12},{8,0},{12,4},{1,9},{5,13},{9,1},{13,5},{2,10},{6,14},... | collective-permute-start | bytes 24584 | tf_op jit(solution)/shard_map/ppermute | solution.py:95
  28.3 13.6 %collective-permute-start.32 = (bf16[128,2048]{1,0:T(8,128)(2,1)S(1)}, bf16[128,2048]{1,0:T(8,128)(2,1)S(1)}, u32[]{:S(2)}, u32[]{:S(2)}) collective-permute-start(bf16[128,2048]{1,0:T(8,128)(2,1)S(1)} %collective-permute-done.28), channel_id=1, source_target_pairs={{0,4},{4,0},{8,12},{12,8},{1,5},{5,1},{9,13},{13,9},{2,6},{6,2},{1... | collective-permute-start | bytes 1572872 | tf_op jit(solution)/shard_map/ppermute | solution.py:95
  41.9 109.4 %collective-permute-start.34 = (bf16[304,4096]{1,0:T(8,128)(2,1)}, bf16[304,4096]{1,0:T(8,128)(2,1)}, u32[]{:S(2)}, u32[]{:S(2)}) collective-permute-start(bf16[304,4096]{1,0:T(8,128)(2,1)} %bitcast_select_fusion), channel_id=1, source_target_pairs={{0,8},{4,12},{8,0},{12,4},{1,9},{5,13},{9,1},{13,5},{2,10},{6,14},... | collective-permute-start | bytes 7471112 | tf_op jit(solution)/shard_map/ppermute | solution.py:95
  42.1 14.9 %collective-permute-start.3 = (bf16[128,2048]{1,0:T(8,128)(2,1)S(1)}, bf16[128,2048]{1,0:T(8,128)(2,1)S(1)}, u32[]{:S(2)}, u32[]{:S(2)}) collective-permute-start(bf16[128,2048]{1,0:T(8,128)(2,1)S(1)} %get-tuple-element.36), channel_id=1, source_target_pairs={{0,2},{2,0},{1,3},{3,1},{4,6},{6,4},{5,7},{7,5},{8,10},{10,8},{9,1... | collective-permute-start | bytes 1572872 | tf_op jit(solution)/shard_map/cond/branch_1_fun/ppermute | solution.py:95
  43.6 14.9 %collective-permute-start.2 = (bf16[128,2048]{1,0:T(8,128)(2,1)S(1)}, bf16[128,2048]{1,0:T(8,128)(2,1)S(1)}, u32[]{:S(2)}, u32[]{:S(2)}) collective-permute-start(bf16[128,2048]{1,0:T(8,128)(2,1)S(1)} %get-tuple-element.36), channel_id=1, source_target_pairs={{0,16},{16,0},{1,17},{17,1},{2,18},{18,2},{3,19},{19,3},{4,20},{20... | collective-permute-start | bytes 1572872 | tf_op jit(solution)/shard_map/cond/branch_1_fun/ppermute | solution.py:95
  45.1 20.9 %collective-permute-start.5 = (bf16[128,2048]{1,0:T(8,128)(2,1)S(1)}, bf16[128,2048]{1,0:T(8,128)(2,1)S(1)}, u32[]{:S(2)}, u32[]{:S(2)}) collective-permute-start(bf16[128,2048]{1,0:T(8,128)(2,1)S(1)} %get-tuple-element.37), channel_id=1, source_target_pairs={{0,2},{2,0},{1,3},{3,1},{4,6},{6,4},{5,7},{7,5},{8,10},{10,8},{9,1... | collective-permute-start | bytes 1572872 | tf_op jit(solution)/shard_map/cond/branch_1_fun/ppermute | solution.py:95
  45.6 21.7 %collective-permute-start.4 = (bf16[128,2048]{1,0:T(8,128)(2,1)S(1)}, bf16[128,2048]{1,0:T(8,128)(2,1)S(1)}, u32[]{:S(2)}, u32[]{:S(2)}) collective-permute-start(bf16[128,2048]{1,0:T(8,128)(2,1)S(1)} %get-tuple-element.37), channel_id=1, source_target_pairs={{0,16},{16,0},{1,17},{17,1},{2,18},{18,2},{3,19},{19,3},{4,20},{20... | collective-permute-start | bytes 1572872 | tf_op jit(solution)/shard_map/cond/branch_1_fun/ppermute | solution.py:95
  67.3 23.0 %collective-permute-start.9 = (bf16[128,2048]{1,0:T(8,128)(2,1)S(1)}, bf16[128,2048]{1,0:T(8,128)(2,1)S(1)}, u32[]{:S(2)}, u32[]{:S(2)}) collective-permute-start(bf16[128,2048]{1,0:T(8,128)(2,1)S(1)} %get-tuple-element.41), channel_id=1, source_target_pairs={{0,2},{2,0},{1,3},{3,1},{4,6},{6,4},{5,7},{7,5},{8,10},{10,8},{9,1... | collective-permute-start | bytes 1572872 | tf_op jit(solution)/shard_map/cond/branch_1_fun/ppermute | solution.py:95
  67.8 22.5 %collective-permute-start.8 = (bf16[128,2048]{1,0:T(8,128)(2,1)S(1)}, bf16[128,2048]{1,0:T(8,128)(2,1)S(1)}, u32[]{:S(2)}, u32[]{:S(2)}) collective-permute-start(bf16[128,2048]{1,0:T(8,128)(2,1)S(1)} %get-tuple-element.41), channel_id=1, source_target_pairs={{0,16},{16,0},{1,17},{17,1},{2,18},{18,2},{3,19},{19,3},{4,20},{20... | collective-permute-start | bytes 1572872 | tf_op jit(solution)/shard_map/cond/branch_1_fun/ppermute | solution.py:95
  69.3 21.0 %collective-permute-start.6 = (bf16[128,2048]{1,0:T(8,128)(2,1)S(1)}, bf16[128,2048]{1,0:T(8,128)(2,1)S(1)}, u32[]{:S(2)}, u32[]{:S(2)}) collective-permute-start(bf16[128,2048]{1,0:T(8,128)(2,1)S(1)} %collective-permute-done.3), channel_id=1, source_target_pairs={{0,16},{16,0},{1,17},{17,1},{2,18},{18,2},{3,19},{19,3},{4,20},{20... | collective-permute-start | bytes 1572872 | tf_op jit(solution)/shard_map/cond/branch_1_fun/ppermute | solution.py:95
  69.9 20.5 %collective-permute-start.7 = (bf16[128,2048]{1,0:T(8,128)(2,1)S(1)}, bf16[128,2048]{1,0:T(8,128)(2,1)S(1)}, u32[]{:S(2)}, u32[]{:S(2)}) collective-permute-start(bf16[128,2048]{1,0:T(8,128)(2,1)S(1)} %collective-permute-done.4), channel_id=1, source_target_pairs={{0,2},{2,0},{1,3},{3,1},{4,6},{6,4},{5,7},{7,5},{8,10},{10,8},{9,1... | collective-permute-start | bytes 1572872 | tf_op jit(solution)/shard_map/cond/branch_1_fun/ppermute | solution.py:95
  94.0 19.0 %collective-permute-start.15 = (bf16[2,4,128,2048]{3,2,1,0:T(8,128)(2,1)}, bf16[2,4,128,2048]{3,2,1,0:T(8,128)(2,1)}, u32[]{:S(2)}, u32[]{:S(2)}) collective-permute-start(bf16[2,4,128,2048]{3,2,1,0:T(8,128)(2,1)} %pad_maximum_fusion.x_ref), channel_id=1, source_target_pairs={{0,1},{1,0},{2,3},{3,2},{4,5},{5,4},{6,7},{7,6},{8,9},{9,8},{10,11... | collective-permute-start | bytes 12582920 | tf_op jit(solution)/shard_map/cond/branch_1_fun/ppermute | solution.py:95
  94.0 15.6 %collective-permute-start.12 = (bf16[384,2048]{1,0:T(8,128)(2,1)}, bf16[384,2048]{1,0:T(8,128)(2,1)}, u32[]{:S(2)}, u32[]{:S(2)}) collective-permute-start(bf16[384,2048]{1,0:T(8,128)(2,1)} %slice_bitcast_fusion), channel_id=1, source_target_pairs={{0,1},{1,0},{2,3},{3,2},{4,5},{5,4},{6,7},{7,6},{8,9},{9,8},{10,11... | collective-permute-start | bytes 4718600 | tf_op jit(solution)/shard_map/cond/branch_1_fun/ppermute | solution.py:95
  94.5 13.9 %collective-permute-start.11 = (bf16[128,2048]{1,0:T(8,128)(2,1)S(1)}, bf16[128,2048]{1,0:T(8,128)(2,1)}, u32[]{:S(2)}, u32[]{:S(2)}) collective-permute-start(bf16[128,2048]{1,0:T(8,128)(2,1)S(1)} %get-tuple-element.44), channel_id=1, source_target_pairs={{0,2},{2,0},{1,3},{3,1},{4,6},{6,4},{5,7},{7,5},{8,10},{10,8},{9,1... | collective-permute-start | bytes 1572872 | tf_op jit(solution)/shard_map/cond/branch_1_fun/ppermute | solution.py:95
  95.9 13.7 %collective-permute-start.10 = (bf16[128,2048]{1,0:T(8,128)(2,1)S(1)}, bf16[128,2048]{1,0:T(8,128)(2,1)}, u32[]{:S(2)}, u32[]{:S(2)}) collective-permute-start(bf16[128,2048]{1,0:T(8,128)(2,1)S(1)} %get-tuple-element.44), channel_id=1, source_target_pairs={{0,16},{16,0},{1,17},{17,1},{2,18},{18,2},{3,19},{19,3},{4,20},{20... | collective-permute-start | bytes 1572872 | tf_op jit(solution)/shard_map/cond/branch_1_fun/ppermute | solution.py:95
  109.6 12.7 %collective-permute-start.14 = (bf16[128,2048]{1,0:T(8,128)(2,1)S(1)}, bf16[128,2048]{1,0:T(8,128)(2,1)S(1)}, u32[]{:S(2)}, u32[]{:S(2)}) collective-permute-start(bf16[128,2048]{1,0:T(8,128)(2,1)S(1)} %copy-done.15), channel_id=1, source_target_pairs={{0,16},{16,0},{1,17},{17,1},{2,18},{18,2},{3,19},{19,3},{4,20},{20... | collective-permute-start | bytes 1572872 | tf_op jit(solution)/shard_map/cond/branch_1_fun/ppermute | solution.py:95
  111.1 12.6 %collective-permute-start.13 = (bf16[128,2048]{1,0:T(8,128)(2,1)}, bf16[128,2048]{1,0:T(8,128)(2,1)S(1)}, u32[]{:S(2)}, u32[]{:S(2)}) collective-permute-start(bf16[128,2048]{1,0:T(8,128)(2,1)} %collective-permute-done.10), channel_id=1, source_target_pairs={{0,2},{2,0},{1,3},{3,1},{4,6},{6,4},{5,7},{7,5},{8,10},{10,8},{9,1... | collective-permute-start | bytes 1572872 | tf_op jit(solution)/shard_map/cond/branch_1_fun/ppermute | solution.py:95
  151.4 111.9 %collective-permute-start.36 = (bf16[384,2048]{1,0:T(8,128)(2,1)}, bf16[384,2048]{1,0:T(8,128)(2,1)}, u32[]{:S(2)}, u32[]{:S(2)}) collective-permute-start(bf16[384,2048]{1,0:T(8,128)(2,1)} %bitcast_select_fusion.2), channel_id=1, source_target_pairs={{0,8},{4,12},{8,0},{12,4},{1,9},{5,13},{9,1},{13,5},{2,10},{6,14},... | collective-permute-start | bytes 4718600 | tf_op jit(solution)/shard_map/ppermute | solution.py:95
  151.4 111.9 %collective-permute-start.35 = (bf16[80,4096]{1,0:T(8,128)(2,1)}, bf16[80,4096]{1,0:T(8,128)(2,1)}, u32[]{:S(2)}, u32[]{:S(2)}) collective-permute-start(bf16[80,4096]{1,0:T(8,128)(2,1)} %bitcast_select_fusion.3), channel_id=1, source_target_pairs={{0,8},{4,12},{8,0},{12,4},{1,9},{5,13},{9,1},{13,5},{2,10},{6,14},... | collective-permute-start | bytes 1966088 | tf_op jit(solution)/shard_map/ppermute | solution.py:95
  154.5 18.4 %collective-permute-start.24 = (bf16[2,4,128,2048]{3,2,1,0:T(8,128)(2,1)}, bf16[2,4,128,2048]{3,2,1,0:T(8,128)(2,1)}, u32[]{:S(2)}, u32[]{:S(2)}) collective-permute-start(bf16[2,4,128,2048]{3,2,1,0:T(8,128)(2,1)} %get-tuple-element.67.x_ref), channel_id=1, source_target_pairs={{0,1},{1,0},{2,3},{3,2},{4,5},{5,4},{6,7},{7,6},{8,9},{9,8},{10,11... | collective-permute-start | bytes 12582920 | tf_op jit(solution)/shard_map/cond/branch_1_fun/ppermute | solution.py:95
  172.9 19.9 %collective-permute-start.20 = (bf16[512,2048]{1,0:T(8,128)(2,1)}, bf16[512,2048]{1,0:T(8,128)(2,1)}, u32[]{:S(2)}, u32[]{:S(2)}) collective-permute-start(bf16[512,2048]{1,0:T(8,128)(2,1)} %down.5), channel_id=1, source_target_pairs={{0,1},{1,0},{2,3},{3,2},{4,5},{5,4},{6,7},{7,6},{8,9},{9,8},{10,11... | collective-permute-start | bytes 6291464 | tf_op jit(solution)/shard_map/cond/branch_1_fun/ppermute | solution.py:95
  178.6 11.5 %collective-permute-start.25 = (bf16[512,384]{1,0:T(8,128)(2,1)S(1)}, bf16[512,384]{1,0:T(8,128)(2,1)S(1)}, u32[]{:S(2)}, u32[]{:S(2)}) collective-permute-start(bf16[512,384]{1,0:T(8,128)(2,1)S(1)} %project.7.own_ref), channel_id=1, source_target_pairs={{0,16},{16,0},{1,17},{17,1},{2,18},{18,2},{3,19},{19,3},{4,20},{20... | collective-permute-start | bytes 1179656 | tf_op jit(solution)/shard_map/cond/branch_1_fun/ppermute | solution.py:95
  192.7 31.5 %collective-permute-start.26 = (bf16[512,2048]{1,0:T(8,128)(2,1)S(1)}, bf16[512,2048]{1,0:T(8,128)(2,1)}, u32[]{:S(2)}, u32[]{:S(2)}) collective-permute-start(bf16[512,2048]{1,0:T(8,128)(2,1)S(1)} %down.7), channel_id=1, source_target_pairs={{0,1},{1,0},{2,3},{3,2},{4,5},{5,4},{6,7},{7,6},{8,9},{9,8},{10,11... | collective-permute-start | bytes 6291464 | tf_op jit(solution)/shard_map/cond/branch_1_fun/ppermute | solution.py:95
  196.8 25.9 %collective-permute-start.21 = (bf16[2,128,2048]{2,1,0:T(8,128)(2,1)}, bf16[2,128,2048]{2,1,0:T(8,128)(2,1)}, u32[]{:S(2)}, u32[]{:S(2)}) collective-permute-start(bf16[2,128,2048]{2,1,0:T(8,128)(2,1)} %bitcast.31), channel_id=1, source_target_pairs={{0,2},{2,0},{1,3},{3,1},{4,6},{6,4},{5,7},{7,5},{8,10},{10,8},{9,1... | collective-permute-start | bytes 3145736 | tf_op jit(solution)/shard_map/cond/branch_1_fun/ppermute | solution.py:95
  197.3 11.2 %collective-permute-start.23 = (bf16[512,384]{1,0:T(8,128)(2,1)S(1)}, bf16[512,384]{1,0:T(8,128)(2,1)S(1)}, u32[]{:S(2)}, u32[]{:S(2)}) collective-permute-start(bf16[512,384]{1,0:T(8,128)(2,1)S(1)} %project.6.own_ref), channel_id=1, source_target_pairs={{0,16},{16,0},{1,17},{17,1},{2,18},{18,2},{3,19},{19,3},{4,20},{20... | collective-permute-start | bytes 1179656 | tf_op jit(solution)/shard_map/cond/branch_1_fun/ppermute | solution.py:95
  226.6 34.5 %collective-permute-start.27 = (bf16[2,128,2048]{2,1,0:T(8,128)(2,1)S(1)}, bf16[2,128,2048]{2,1,0:T(8,128)(2,1)S(1)}, u32[]{:S(2)}, u32[]{:S(2)}) collective-permute-start(bf16[2,128,2048]{2,1,0:T(8,128)(2,1)S(1)} %bitcast.93), channel_id=1, source_target_pairs={{0,2},{2,0},{1,3},{3,1},{4,6},{6,4},{5,7},{7,5},{8,10},{10,8},{9,1... | collective-permute-start | bytes 3145736 | tf_op jit(solution)/shard_map/cond/branch_1_fun/ppermute | solution.py:95
  227.2 32.9 %collective-permute-start.22 = (bf16[128,2048]{1,0:T(8,128)(2,1)S(1)}, bf16[128,2048]{1,0:T(8,128)(2,1)S(1)}, u32[]{:S(2)}, u32[]{:S(2)}) collective-permute-start(bf16[128,2048]{1,0:T(8,128)(2,1)S(1)} %slice_bitcast_fusion.2), channel_id=1, source_target_pairs={{0,4},{4,0},{8,12},{12,8},{1,5},{5,1},{9,13},{13,9},{2,6},{6,2},{1... | collective-permute-start | bytes 1572872 | tf_op jit(solution)/shard_map/cond/branch_1_fun/ppermute | solution.py:95
  264.8 26.2 %collective-permute-start.37 = (bf16[128,2048]{1,0:T(8,128)(2,1)}, bf16[128,2048]{1,0:T(8,128)(2,1)S(1)}, u32[]{:S(2)}, u32[]{:S(2)}) collective-permute-start(bf16[128,2048]{1,0:T(8,128)(2,1)} %get-tuple-element.144), channel_id=1, source_target_pairs={{0,8},{4,12},{8,0},{12,4},{1,9},{5,13},{9,1},{13,5},{2,10},{6,14},... | collective-permute-start | bytes 1572872 | tf_op jit(solution)/shard_map/ppermute | solution.py:95
  264.9 26.3 %collective-permute-start.38 = (bf16[128,2048]{1,0:T(8,128)(2,1)}, bf16[128,2048]{1,0:T(8,128)(2,1)}, u32[]{:S(2)}, u32[]{:S(2)}) collective-permute-start(bf16[128,2048]{1,0:T(8,128)(2,1)} %get-tuple-element.145), channel_id=1, source_target_pairs={{0,4},{4,0},{8,12},{12,8},{1,5},{5,1},{9,13},{13,9},{2,6},{6,2},{1... | collective-permute-start | bytes 1572872 | tf_op jit(solution)/shard_map/ppermute | solution.py:95
  (30 other events, 428.0 us)
